TPU v7x, 128 devices: a whole 4x4x4 slice. The times are simulated.
128 devices in a mesh: rep: 2 (over core), shard: 64 (over y, x, z).
Axes of the slice: x: 4, y: 4, z: 4, core: 2. Of those that a mesh axis runs over, the one named last changes fastest.
Arguments:
- table_rows: float32 [131072, 128], P('shard'), may hold values from -3 to 3
- accum: float32 [131072, 128], P('shard'), may hold values from 0.1 to 1
- hash_keys: int32 [131072], P('shard'), may hold values from 0 to 131071, as said below
- hash_place: int32 [131072], replicated, may hold values from 0 to 131071, as said below
- sample_ids: int32 [32768, 32], P(('rep', 'shard')), may hold values from 0 to 131071, as said below
- sample_grads: bfloat16 [32768, 1024], P(('rep', 'shard')), may hold values from -6 to 6
- req_ids: int32 [16384, 32], P(('rep', 'shard')), may hold values from 0 to 131071, as said below
- w_hidden: bfloat16 [1024, 1024], replicated, may hold values from -0.1875 to 0.1875
- b_hidden: float32 [1024], replicated, may hold values from -3 to 3
- w_score: bfloat16 [1024], replicated, may hold values from -0.1875 to 0.1875
Outputs:
- new_rows: float32 [131072, 128], P('shard')
- new_accum: float32 [131072, 128], P('shard')
- serving_rows: bfloat16 [131072, 128], P('shard')
- scores: float32 [16384], P(('rep', 'shard'))
Inputs may be any that keep to these rules, and one draw needn't show every extreme that they name: `hash_keys`: A permutation of the keys; the trainer row p holds a key k with k // 2048 == (p % 2048) // 32. The inverse of hash_keys: hash_keys[hash_place[k]] == k. `sample_ids`: among one device's samples, at most 256 ids have a trainer row in one shard's block of 2048 rows, and this count is reached on every device. `req_ids`: among one device's requests, at most 128 ids lie in one block of 2048 consecutive keys, and this count is reached on every device.
All inputs are finite; a program needn't handle non-finite values.
Results may differ from a plain program's by a relative error of at most 0.0064.
Values may be sent and summed in bfloat16 or wider, within the bound.
No kernel may reach another device: no remote copies, remote signals or barrier semaphores. Data moves between devices by JAX's collectives and lax.ppermute only.
A program may use at most 128 MiB of HBM per device.

v0:
```python
import functools

import jax
import jax.numpy as jnp
from jax import lax
from jax.experimental import pallas as pl
from jax.experimental.pallas import tpu as pltpu
from jax.sharding import PartitionSpec as P

F32, BF16, I32 = jnp.float32, jnp.bfloat16, jnp.int32
NT = (((1,), (1,)), ((), ()))
VMEM_LIMIT = 56 * 2**20
EXTRA = 16


def params():
    return pltpu.CompilerParams(vmem_limit_bytes=VMEM_LIMIT)


def iota(shape, axis, dtype=I32):
    return lax.broadcasted_iota(I32, shape, axis).astype(dtype)


def dot(a, b):
    return jnp.dot(a, b, preferred_element_type=F32)


def dot_nt(a, b):
    return lax.dot_general(a, b, NT, preferred_element_type=F32)


def ones_where(mask):
    return jnp.where(mask, 1.0, 0.0).astype(BF16)


def rank_chunk(owner, base, shards, tri, ones):
    count = owner.shape[1]
    own = jnp.where(iota((shards, count), 0, F32) == owner, 1.0, 0.0)
    own_b = own.astype(BF16)
    before = dot(own_b, tri) + jnp.concatenate([base] * (count // 128), axis=1)
    return own, jnp.sum(own * before, axis=0, keepdims=True), base + dot(own_b, ones)


def index_kernel(shards, rows_dev, ids_ref, place_ref, req_ref, col_ref, extra_ref, mslot_ref, ex):
    block = rows_dev // shards
    shift = rows_dev.bit_length() - 1
    place = place_ref[...]
    table = jnp.concatenate(
        [(place >> shift).astype(F32).T, (place & (block - 1)).astype(F32).T], axis=0
    ).astype(BF16)
    highs = place_ref.shape[0]
    width = ids_ref.shape[1]
    tri = ones_where(iota((width, width), 0) < iota((width, width), 1))
    ones = jnp.ones((width, 128), BF16)
    lane = iota((1, width), 1)

    def train(c, carry):
        base, col, row = carry
        ids = ids_ref[pl.ds(c, 1), :]
        hot = ones_where(iota((highs, width), 0) == (ids >> 7))
        both = dot(table, hot)
        mask = iota((128, width), 0) == (ids & 127)
        owner = jnp.sum(jnp.where(mask, both[:128], 0.0), axis=0, keepdims=True)
        place_low = jnp.sum(jnp.where(mask, both[128:], 0.0), axis=0, keepdims=True)
        own, rank, base = rank_chunk(owner, base, shards, tri, ones)
        at = ones_where(iota((width, width), 0, F32) == rank)
        field = (c // 4 + 1).astype(F32)
        source = jnp.concatenate([own * lane.astype(F32), own * field], axis=0).astype(BF16)
        target = jnp.concatenate([own * (ids >> shift).astype(F32), own * place_low], axis=0)
        col = col + dot_nt(at, source)
        row = row + dot_nt(target.astype(BF16), at)
        return base, col, row

    base = jnp.zeros((shards, 128), F32)
    unused, col, row = lax.fori_loop(
        0,
        ids_ref.shape[0],
        train,
        (base, jnp.zeros((width, 2 * shards), F32), jnp.zeros((2 * shards, width), F32)),
    )
    col_ref[...] = col

    def serve(c, carry):
        base, row = carry
        ids = req_ref[pl.ds(c, 1), :]
        local = ids & (rows_dev - 1)
        own, rank, base = rank_chunk((ids >> shift).astype(F32), base, shards, tri, ones)
        at = ones_where(iota((128, width), 0, F32) == rank)
        digits = [
            own * (local >> 5).astype(F32),
            own * (local & 31).astype(F32),
            own * (lane & 127).astype(F32),
            own * (c // 2 + 1).astype(F32),
        ]
        row = row + dot_nt(jnp.concatenate(digits, axis=0).astype(BF16), at)
        return base, row

    unused, asked = lax.fori_loop(
        0, req_ref.shape[0], serve, (base, jnp.zeros((4 * shards, 128), F32))
    )
    ex[...] = jnp.zeros_like(ex)
    parts = [
        row[:shards, :128],
        row[:shards, 128:],
        row[shards:, :128],
        row[shards:, 128:],
        asked[:shards],
        asked[shards : 2 * shards],
    ]
    for kind, part in enumerate(parts):
        ex[pl.ds(kind, shards, stride=EXTRA), :] = part
    extra_ref[...] = ex[...].astype(BF16)
    query = asked[2 * shards : 3 * shards] + (asked[3 * shards :] - 1.0) * 128.0
    mslot_ref[...] = query.astype(I32)


def build_kernel(group, shards, col_ref, grads_ref, extra_ref, out_ref):
    slots = col_ref.shape[0]
    samples = grads_ref.shape[0]
    fields = grads_ref.shape[1] // 128

    def one(b, unused):
        owner = pl.program_id(0) * group + b
        turned = pltpu.roll(col_ref[...], lax.rem(2 * shards - owner, 2 * shards), 1)
        source = turned[:, 0:1]
        field = jnp.broadcast_to(turned[:, shards : shards + 1], (slots, 128))
        hot = ones_where(iota((slots, samples), 1, F32) == source)
        rows = dot(hot, grads_ref[...])
        picked = jnp.zeros((slots, 128), F32)
        for f in range(fields):
            picked = jnp.where(field == f + 1.0, rows[:, f * 128 : (f + 1) * 128], picked)
        out_ref[b, 0:slots, :] = picked.astype(BF16)
        out_ref[b, slots : slots + EXTRA, :] = extra_ref[pl.ds(b * EXTRA, EXTRA), :]
        return unused

    lax.fori_loop(0, group, one, 0)


def sum_kernel(group, got_ref, extra_ref, out_ref, scr, hi_scr, lo_scr, total):
    shards = extra_ref.shape[0]
    slots = got_ref.shape[1] - EXTRA
    step = pl.program_id(0)

    @pl.when(step == 0)
    def _():
        scr[...] = extra_ref[...].astype(F32).reshape(scr.shape)
        lows = []
        for half in range(2):
            ranges = scr[pl.ds(half, shards, stride=EXTRA), :].astype(I32)
            within = scr[pl.ds(2 + half, shards, stride=EXTRA), :].astype(I32)
            hi_scr[half] = (ranges & 15) * 32 + within
            lows.append((ranges >> 4).astype(F32))
        lo_scr[...] = jnp.concatenate(lows, axis=0).T
        total[...] = jnp.zeros_like(total)

    highs, values = [], []
    for k in range(group):
        src = step * group + k
        hi = jnp.concatenate([hi_scr[0, pl.ds(src, 1), :], hi_scr[1, pl.ds(src, 1), :]], axis=1)
        highs.append(ones_where(iota((512, slots), 0) == hi))
        turned = pltpu.roll(lo_scr[...], lax.rem(2 * shards - src, 2 * shards), 1)
        low = jnp.concatenate([turned[:, 0:1], turned[:, shards : shards + 1]], axis=0)
        low = jnp.broadcast_to(low, (slots, 128))
        rows = got_ref[k, 0:slots, :]
        values.append(
            jnp.concatenate([rows * ones_where(low == float(q)) for q in range(4)], axis=1)
        )
    total[...] += dot(jnp.concatenate(highs, axis=1), jnp.concatenate(values, axis=0))

    @pl.when(step == pl.num_programs(0) - 1)
    def _():
        for q in range(4):
            out_ref[q * 512 : (q + 1) * 512, :] = total[:, q * 128 : (q + 1) * 128]


def take_rows(low, high, wide):
    count = low.shape[0]
    rows = dot(ones_where(iota((count, 512), 1, F32) == high), wide)
    low = jnp.broadcast_to(low, (count, 128))
    picked = rows[:, 0:128]
    for q in range(1, 4):
        picked = jnp.where(low == float(q), rows[:, q * 128 : (q + 1) * 128], picked)
    return picked.astype(BF16)


def widen(rows):
    return jnp.concatenate([rows[q * 512 : (q + 1) * 512] for q in range(4)], axis=1)


def serve_kernel(group, moved_ref, place_ref, extra_ref, serving_ref, found_ref, scr, wide, low_scr, high_scr):
    shards = extra_ref.shape[0]
    step = pl.program_id(0)

    @pl.when(step == 0)
    def _():
        place = place_ref[...]
        owner = place >> 11
        low = (owner >> 4).astype(F32).T
        high = ((owner & 15) * 32 + (place & 31)).astype(F32).T
        moved = widen(moved_ref[...])
        for b in range(place.shape[0]):
            serving_ref[b * 128 : (b + 1) * 128, :] = take_rows(
                low[:, b : b + 1], high[:, b : b + 1], moved
            )
        wide[...] = widen(serving_ref[...])
        scr[...] = extra_ref[...].astype(F32).reshape(scr.shape)
        first = scr[pl.ds(4, shards, stride=EXTRA), :].astype(I32)
        second = scr[pl.ds(5, shards, stride=EXTRA), :].astype(I32)
        zero = jnp.zeros((128 - shards, 128), F32)
        low_scr[...] = jnp.concatenate([(first >> 4).astype(F32), zero], axis=0).T
        high_scr[...] = jnp.concatenate(
            [((first & 15) * 32 + second).astype(F32), zero], axis=0
        ).T

    turn = lax.rem(128 - step * group, 128)
    low = pltpu.roll(low_scr[...], turn, 1)
    high = pltpu.roll(high_scr[...], turn, 1)
    for b in range(group):
        found_ref[b] = take_rows(low[:, b : b + 1], high[:, b : b + 1], wide[...])


def rank_kernel(group, ret_ref, mslot_ref, w_ref, b_ref, score_ref, out_ref, total):
    step = pl.program_id(0)
    queries = total.shape[0]

    @pl.when(step == 0)
    def _():
        total[...] = jnp.zeros_like(total)

    slots = ret_ref.shape[1]
    hots = [
        ones_where(iota((queries, slots), 0) == mslot_ref[pl.ds(step * group + b, 1), :])
        for b in range(group)
    ]
    total[...] += dot(jnp.concatenate(hots, axis=1), ret_ref[...].reshape(group * slots, 128))

    @pl.when(step == pl.num_programs(0) - 1)
    def _():
        rows = out_ref.shape[1]
        pooled = jnp.concatenate(
            [total[f * rows : (f + 1) * rows, :] for f in range(queries // rows)], axis=1
        ).astype(BF16)
        hidden = jnp.maximum(dot(pooled, w_ref[...]) + b_ref[...], 0.0).astype(BF16)
        out_ref[...] = dot_nt(score_ref[...], hidden)


def adagrad_step(weights, history, gradient):
    updated = history + gradient * gradient
    return (weights - 0.1 * gradient * lax.rsqrt(updated), updated)


def whole(shape):
    return pl.BlockSpec(shape, lambda *step: (0,) * len(shape))


def on_device(
    table_rows,
    accum,
    hash_keys,
    hash_place,
    sample_ids,
    sample_grads,
    req_ids,
    w_hidden,
    b_hidden,
    w_score,
):
    rows_dev, row_width = table_rows.shape
    shards = lax.axis_size("shard")
    samples, id_columns = sample_ids.shape
    requests = req_ids.shape[0]
    slots = 2 * samples * id_columns // shards
    req_slots = 2 * requests * id_columns // shards
    fields = sample_grads.shape[1] // row_width
    hidden_width = w_hidden.shape[1]
    places = hash_place.reshape(-1, 128)
    shape = jax.ShapeDtypeStruct

    col, extra, mslot = pl.pallas_call(
        functools.partial(index_kernel, shards, rows_dev),
        out_shape=(
            shape((slots, 2 * shards), F32),
            shape((shards * EXTRA, 128), BF16),
            shape((shards, req_slots), I32),
        ),
        scratch_shapes=[pltpu.VMEM((shards * EXTRA, 128), F32)],
        compiler_params=params(),
        name="index",
    )(sample_ids.T, places, req_ids.T.reshape(-1, 2 * requests))

    group = 8
    sent = pl.pallas_call(
        functools.partial(build_kernel, group, shards),
        grid=(shards // group,),
        in_specs=[
            whole((slots, 2 * shards)),
            whole(sample_grads.shape),
            pl.BlockSpec((group * EXTRA, 128), lambda g: (g, 0)),
        ],
        out_specs=pl.BlockSpec((group, slots + EXTRA, row_width), lambda g: (g, 0, 0)),
        out_shape=shape((shards, slots + EXTRA, row_width), BF16),
        compiler_params=params(),
        name="build",
    )(col, sample_grads, extra)
    got = lax.all_to_all(sent, "shard", split_axis=0, concat_axis=0, tiled=True)

    group = 4
    extra_spec = pl.BlockSpec((shards, EXTRA, row_width), lambda g: (0, slots // EXTRA, 0))
    partial_sum = pl.pallas_call(
        functools.partial(sum_kernel, group),
        grid=(shards // group,),
        in_specs=[
            pl.BlockSpec((group, slots + EXTRA, row_width), lambda g: (g, 0, 0)),
            extra_spec,
        ],
        out_specs=whole((rows_dev, row_width)),
        out_shape=shape((rows_dev, row_width), F32),
        scratch_shapes=[
            pltpu.VMEM((shards * EXTRA, 128), F32),
            pltpu.VMEM((2, shards, 128), I32),
            pltpu.VMEM((128, 128), F32),
            pltpu.VMEM((512, 512), F32),
        ],
        compiler_params=params(),
        name="gradient_sum",
    )(got, got)
    other = lax.ppermute(partial_sum, "rep", [(0, 1), (1, 0)])
    new_rows, new_accum = adagrad_step(table_rows, accum, partial_sum + other)
    moved = lax.all_to_all(
        new_rows.astype(BF16).reshape(shards, rows_dev // shards, row_width),
        "shard",
        split_axis=0,
        concat_axis=0,
        tiled=True,
    ).reshape(rows_dev, row_width)

    place_rows = rows_dev // 128
    own_places = lax.dynamic_slice_in_dim(
        places, lax.axis_index("shard") * place_rows, place_rows, axis=0
    )
    group = 8
    serving_rows, found = pl.pallas_call(
        functools.partial(serve_kernel, group),
        grid=(shards // group,),
        in_specs=[whole(moved.shape), whole((place_rows, 128)), extra_spec],
        out_specs=(
            whole((rows_dev, row_width)),
            pl.BlockSpec((group, req_slots, row_width), lambda g: (g, 0, 0)),
        ),
        out_shape=(
            shape((rows_dev, row_width), BF16),
            shape((shards, req_slots, row_width), BF16),
        ),
        scratch_shapes=[
            pltpu.VMEM((shards * EXTRA, 128), F32),
            pltpu.VMEM((512, 512), BF16),
            pltpu.VMEM((128, 128), F32),
            pltpu.VMEM((128, 128), F32),
        ],
        compiler_params=params(),
        name="serve",
    )(moved, own_places, got)
    returned = lax.all_to_all(found, "shard", split_axis=0, concat_axis=0, tiled=True)

    scores = pl.pallas_call(
        functools.partial(rank_kernel, group),
        grid=(shards // group,),
        in_specs=[
            pl.BlockSpec((group, req_slots, row_width), lambda g: (g, 0, 0)),
            whole((shards, req_slots)),
            whole(w_hidden.shape),
            whole((1, hidden_width)),
            whole((1, hidden_width)),
        ],
        out_specs=whole((1, requests)),
        out_shape=shape((1, requests), F32),
        scratch_shapes=[pltpu.VMEM((requests * fields, row_width), F32)],
        compiler_params=params(),
        name="pool_rank",
    )(returned, mslot, w_hidden, b_hidden.reshape(1, -1), w_score.reshape(1, -1))
    return (new_rows, new_accum, serving_rows, scores.reshape(requests))


def solution(mesh):
    return jax.shard_map(
        on_device,
        mesh=mesh,
        in_specs=(
            P("shard", None),
            P("shard", None),
            P("shard"),
            P(),
            P(("rep", "shard"), None),
            P(("rep", "shard"), None),
            P(("rep", "shard"), None),
            P(),
            P(),
            P(),
        ),
        out_specs=(P("shard", None), P("shard", None), P("shard", None), P(("rep", "shard"))),
        check_vma=False,
    )
```

profile of v0, /device:TPU:0, one launch (start us, length us, event | category | flops | bytes accessed | tf_op | source)
XLA Modules:
  0.0 233.2 jit_solution(9739992823928767419)
XLA Ops:
  0.6 1.3 reshape.30.req_ref
  2.0 33.0 %index.1 = (f32[256,128]{1,0:T(8,128)}, bf16[1024,128]{1,0:T(8,128)(2,1)}, s32[64,128]{1,0:T(8,128)}) custom-call(s32[32,256]{1,0:T(8,128)} %bitcast.10, s32[1024,128]{1,0:T(8,128)} %bitcast.8, s32[16,256]{1,0:T(8,128)} %reshape.30.req_ref), custom_call_target="tpu_custom_call" | custom-call | tf_op jit(solution)/shard_map/index/pallas_call | solution.py:279
  35.0 31.3 %build.1 = bf16[64,272,128]{2,1,0:T(8,128)(2,1)} custom-call(f32[256,128]{1,0:T(8,128)} %get-tuple-element.9.col_ref, bf16[256,1024]{1,0:T(8,128)(2,1)} %grads_ref.1, bf16[1024,128]{1,0:T(8,128)(2,1)} %get-tuple-element.10.extra_ref), custom_call_target="tpu_custom_call" | custom-call | tf_op jit(solution)/shard_map/build/pallas_call | solution.py:292
  66.2 67.1 %all_to_all.15.got_ref.extra_ref = bf16[64,272,128]{2,1,0:T(8,128)(2,1)} all-to-all(bf16[64,272,128]{2,1,0:T(8,128)(2,1)} %build.1), channel_id=1, replica_groups=mesh['rep'=2,'shard'=64] {'shard'}, dimensions={0} | all-to-all | bytes 8912896 | tf_op jit(solution)/shard_map/all_to_all | solution.py:305
  133.3 0.0 copy-start.2
  133.3 0.0 copy-start.3
  133.3 19.9 %gradient_sum.1 = f32[2048,128]{1,0:T(8,128)} custom-call(bf16[64,272,128]{2,1,0:T(8,128)(2,1)} %all_to_all.15.got_ref.extra_ref, bf16[64,272,128]{2,1,0:T(8,128)(2,1)} %all_to_all.15.got_ref.extra_ref), custom_call_target="tpu_custom_call" | custom-call | tf_op jit(solution)/shard_map/gradient_sum/pallas_call | solution.py:309
  153.2 0.0 collective-permute-start
  153.2 2.9 %collective-permute-done = f32[2048,128]{1,0:T(8,128)S(1)} collective-permute-done((f32[2048,128]{1,0:T(8,128)}, f32[2048,128]{1,0:T(8,128)S(1)}, u32[]{:S(2)}, u32[]{:S(2)}) %collective-permute-start) | collective-permute-done | bytes 1048608 | tf_op jit(solution)/shard_map/ppermute | solution.py:327
  156.1 0.0 copy-done.2
  156.1 0.0 copy-done.3
  156.1 3.0 %fusion = (bf16[2048,128]{1,0:T(8,128)(2,1)}, f32[2048,128]{1,0:T(8,128)}, f32[2048,128]{1,0:T(8,128)}) fusion(f32[2048,128]{1,0:T(8,128)S(1)} %copy-done.2, f32[2048,128]{1,0:T(8,128)} %gradient_sum.1, f32[2048,128]{1,0:T(8,128)S(1)} %collective-permute-done, f32[2048,128]{1,0:T(8,128)S(1)} %copy-done.3), kind=kLoop, calls=%fused_computation.3 | loop fusion | flops 1835008 | bytes 6815744 | tf_op jit(solution)/shard_map/convert_element_type | solution.py:330
  159.1 5.2 %all-to-all-start.1 = ((bf16[64,32,128]{2,1,0:T(8,128)(2,1)}), bf16[64,32,128]{2,1,0:T(8,128)(2,1)S(1)}, u32[]{:S(2)}, u32[]{:S(2)}) async-start(bf16[64,32,128]{2,1,0:T(8,128)(2,1)} %bitcast.3), calls=%async_computation.1 | async-start | bytes 1048576 | tf_op jit(solution)/shard_map/all_to_all | solution.py:329
  164.3 1.3 constant_dynamic-slice_fusion.place_ref
  165.6 12.3 %all-to-all-done.1 = bf16[64,32,128]{2,1,0:T(8,128)(2,1)S(1)} async-done(((bf16[64,32,128]{2,1,0:T(8,128)(2,1)}), bf16[64,32,128]{2,1,0:T(8,128)(2,1)S(1)}, u32[]{:S(2)}, u32[]{:S(2)}) %all-to-all-start.1) | async-done | bytes 524320 | tf_op jit(solution)/shard_map/all_to_all | solution.py:329
  177.9 0.0 copy-start.1
  177.9 0.8 copy-done.1
  178.7 10.4 %serve.1 = (bf16[2048,128]{1,0:T(8,128)(2,1)}, bf16[64,128,128]{2,1,0:T(8,128)(2,1)}) custom-call(bf16[2048,128]{1,0:T(8,128)(2,1)} %bitcast.7, s32[16,128]{1,0:T(8,128)} %constant_dynamic-slice_fusion.place_ref, bf16[64,272,128]{2,1,0:T(8,128)(2,1)} %all_to_all.15.got_ref.extra_ref), custom_call_target="tpu_custom_call" | custom-call | tf_op jit(solution)/shard_map/serve/pallas_call | solution.py:342
  189.0 0.0 copy-start.4
  189.0 5.0 %all-to-all-start.2 = ((bf16[64,128,128]{2,1,0:T(8,128)(2,1)}), bf16[64,128,128]{2,1,0:T(8,128)(2,1)S(1)}, u32[]{:S(2)}, u32[]{:S(2)}) async-start(bf16[64,128,128]{2,1,0:T(8,128)(2,1)} %get-tuple-element.12), calls=%async_computation.2 | async-start | bytes 4194304 | tf_op jit(solution)/shard_map/all_to_all | solution.py:363
  194.0 0.0 copy-done.4
  194.0 0.6 reshape.34.score_ref
  194.6 27.9 %all-to-all-done.2.ret_ref = bf16[64,128,128]{2,1,0:T(8,128)(2,1)S(1)} async-done(((bf16[64,128,128]{2,1,0:T(8,128)(2,1)}), bf16[64,128,128]{2,1,0:T(8,128)(2,1)S(1)}, u32[]{:S(2)}, u32[]{:S(2)}) %all-to-all-start.2) | async-done | bytes 2097184 | tf_op jit(solution)/shard_map/all_to_all | solution.py:363
  222.5 0.0 copy-start
  222.5 1.3 copy-done
  223.8 9.4 %pool_rank.1 = f32[1,128]{1,0:T(1,128)} custom-call(bf16[64,128,128]{2,1,0:T(8,128)(2,1)} %copy-done, s32[64,128]{1,0:T(8,128)} %get-tuple-element.13.mslot_ref, bf16[1024,1024]{1,0:T(8,128)(2,1)} %w_ref.1, f32[1,1024]{1,0:T(1,128)} %bitcast.12, bf16[1,1024]{1,0:T(2,128)(2,1)} %reshape.34.score_ref), custom_call_target="tpu_custom_call" | custom-call | tf_op jit(solution)/shard_map/pool_rank/pallas_call | solution.py:365
Async XLA Ops:
  133.3 22.8 %copy-start.2 = (f32[2048,128]{1,0:T(8,128)S(1)}, f32[2048,128]{1,0:T(8,128)}, u32[]{:S(2)}) copy-start(f32[2048,128]{1,0:T(8,128)} %param.10) | copy-start | bytes 3145732
  133.3 22.8 %copy-start.3 = (f32[2048,128]{1,0:T(8,128)S(1)}, f32[2048,128]{1,0:T(8,128)}, u32[]{:S(2)}) copy-start(f32[2048,128]{1,0:T(8,128)} %param.11) | copy-start | bytes 3145732
  153.2 2.9 %collective-permute-start = (f32[2048,128]{1,0:T(8,128)}, f32[2048,128]{1,0:T(8,128)S(1)}, u32[]{:S(2)}, u32[]{:S(2)}) collective-permute-start(f32[2048,128]{1,0:T(8,128)} %gradient_sum.1), channel_id=1, source_target_pairs={{0,64},{64,0},{1,65},{65,1},{2,66},{66,2},{3,67},{67,3},{4,68},{68... | collective-permute-start | bytes 3145736 | tf_op jit(solution)/shard_map/ppermute | solution.py:327
  159.1 18.8 %all-to-all-start.1 = ((bf16[64,32,128]{2,1,0:T(8,128)(2,1)}), bf16[64,32,128]{2,1,0:T(8,128)(2,1)S(1)}, u32[]{:S(2)}, u32[]{:S(2)}) async-start(bf16[64,32,128]{2,1,0:T(8,128)(2,1)} %bitcast.3), calls=%async_computation.1 | async-start | bytes 1048576 | tf_op jit(solution)/shard_map/all_to_all | solution.py:329
  177.9 0.8 copy-start.1
  189.0 5.0 %copy-start.4 = (bf16[1024]{0:T(1024)(128)(2,1)S(1)}, bf16[1024]{0:T(1024)(128)(2,1)}, u32[]{:S(2)}) copy-start(bf16[1024]{0:T(1024)(128)(2,1)} %param.18) | copy-start | bytes 6148
  189.0 33.5 %all-to-all-start.2 = ((bf16[64,128,128]{2,1,0:T(8,128)(2,1)}), bf16[64,128,128]{2,1,0:T(8,128)(2,1)S(1)}, u32[]{:S(2)}, u32[]{:S(2)}) async-start(bf16[64,128,128]{2,1,0:T(8,128)(2,1)} %get-tuple-element.12), calls=%async_computation.2 | async-start | bytes 4194304 | tf_op jit(solution)/shard_map/all_to_all | solution.py:363
  222.5 1.3 copy-start
where the time goes:
time: 234 us; the launch traced here: 233 us
  Pallas kernels  104 us (44%)
  blocking collectives  67.1 us (29%)
  waiting for transfers between devices  43 us (18%)
  starting transfers between devices  10.1 us (4%)
  local copies, waits for them, and re-layouts  5.38 us (2%)
  other arithmetic  3 us (1%)
    all_to_all x1, blocking collectives, on_device(): got = lax.all_to_all(sent, 'shard', split_axis=0, concat_axis=0, tiled=True)  67.1 us
    pallas_call x1, Pallas kernels, on_device(): pl.pallas_call(functools.partial(index_kernel, shards, rows_dev), out_sha...  33 us
    pallas_call x1, Pallas kernels, on_device(): pl.pallas_call(functools.partial(build_kernel, group, shards), grid=(shar...  31.3 us
    all_to_all x1, waiting for transfers between devices, on_device(): lax.all_to_all(found, 'shard', split_axis=0, concat_axis=0, tiled=True)  27.9 us
    pallas_call x1, Pallas kernels, on_device(): pl.pallas_call(functools.partial(sum_kernel, group), grid=(shards // grou...  19.9 us
    all_to_all x1, waiting for transfers between devices, on_device(): lax.all_to_all(new_rows.astype(BF16).reshape(shards, rows_dev // shards,...  12.3 us
    pallas_call x1, Pallas kernels, on_device(): pl.pallas_call(functools.partial(serve_kernel, group), grid=(shards // gr...  10.4 us
    pallas_call x1, Pallas kernels, on_device(): pl.pallas_call(functools.partial(rank_kernel, group), grid=(shards // gro...  9.37 us
  transfers between devices with their start and end apart: 3, of which 3 were waited for; matrix products, arithmetic and copies ran while one was open for 1% of the time, Pallas kernels for 0%

commit v1 on v0

v1 whole, which is shorter than its diff:
```python
import functools

import jax
import jax.numpy as jnp
from jax import lax
from jax.experimental import pallas as pl
from jax.experimental.pallas import tpu as pltpu
from jax.sharding import PartitionSpec as P

F32, BF16, I32 = jnp.float32, jnp.bfloat16, jnp.int32
NT = (((1,), (1,)), ((), ()))
VMEM_LIMIT = 60 * 2**20
EXTRA = 16
LANES = 128


def iota(shape, axis, dtype=I32):
    return lax.broadcasted_iota(I32, shape, axis).astype(dtype)


def dot(a, b):
    return jnp.dot(a, b, preferred_element_type=F32)


def dot_nt(a, b):
    return lax.dot_general(a, b, NT, preferred_element_type=F32)


def ones_where(mask):
    return jnp.where(mask, 1.0, 0.0).astype(BF16)


def lanes_of(ref, first, count):
    return jnp.concatenate([ref[pl.ds(first + k, 1), :] for k in range(count)], axis=1)


def rank_ids(owner, base, shards, tri, ones):
    width = tri.shape[0]
    chunks = owner.shape[1] // width
    own = jnp.where(iota((shards, owner.shape[1]), 0, F32) == owner, 1.0, 0.0)
    stacked = jnp.concatenate(
        [own[:, k * width : (k + 1) * width] for k in range(chunks)], axis=0
    ).astype(BF16)
    before = dot(stacked, tri)
    totals = dot(stacked, ones)
    ranks = []
    for k in range(chunks):
        rows = slice(k * shards, (k + 1) * shards)
        at = before[rows] + jnp.concatenate([base] * (width // LANES), axis=1)
        ranks.append(jnp.sum(own[:, k * width : (k + 1) * width] * at, axis=0, keepdims=True))
        base = base + totals[rows]
    return own, jnp.concatenate(ranks, axis=1), base


def strict_upper(width):
    return ones_where(iota((width, width), 0) < iota((width, width), 1))


def pack_places(place, shift, block):
    last = place & (block - 1)
    scale = (1 << (last & 15)).astype(F32) * jnp.where(last >= 16, 65536.0, 1.0)
    packed = ((place >> shift) + 64).astype(F32) * scale
    half = place.shape[0] // 2
    return jnp.concatenate([packed[:half].T, packed[half:].T], axis=0).astype(BF16)


def look_up(table, ids):
    count = ids.shape[1]
    lows, lines = table.shape
    line = ids >> 7
    hot = ones_where(iota((lines, count), 0) == (line & (lines - 1)))
    low = (ids & 127) + jnp.where(line >= lines, LANES, 0)
    found = jnp.where(iota((lows, count), 0) == low, dot(table, hot), 0.0)
    value = jnp.sum(found, axis=0, keepdims=True)
    last = jnp.zeros_like(value)
    for bits in (16, 8, 4, 2, 1):
        big = value >= 64.0 * 2.0**bits
        value = jnp.where(big, value * 2.0**-bits, value)
        last = last + jnp.where(big, float(bits), 0.0)
    return value - 64.0, last


def index_kernel(
    shards, rows_dev, per_field, groups,
    ids_ref, place_ref, col_ref, off_ref, extra_ref, table, ex, own_scr, rank_scr, mark, off_scr,
):
    shift = rows_dev.bit_length() - 1
    width = ids_ref.shape[1]
    count = per_field * width
    fields = ids_ref.shape[0] // per_field
    span = fields // groups
    table[...] = pack_places(place_ref[...], shift, rows_dev // shards)
    tri = strict_upper(width)
    ones = jnp.ones((width, LANES), BF16)

    def field_step(field, carry):
        base, row = carry
        ids = lanes_of(ids_ref, field * per_field, per_field)
        owner, last = look_up(table[...], ids)
        mark[pl.ds(field * shards, shards), :] = base
        own, rank, base = rank_ids(owner, base, shards, tri, ones)
        own_scr[pl.ds(field, 1), :] = owner
        rank_scr[pl.ds(field, 1), :] = rank
        at = ones_where(iota((width, count), 0, F32) == rank)
        target = jnp.concatenate([own * (ids >> shift).astype(F32), own * last], axis=0)
        row = row + dot_nt(target.astype(BF16), at)
        return base, row

    base, row = lax.fori_loop(
        0,
        fields,
        field_step,
        (jnp.zeros((shards, LANES), F32), jnp.zeros((2 * shards, width), F32)),
    )
    mark[fields * shards :, :] = base
    ex[...] = jnp.zeros_like(ex)
    for kind in range(2):
        for half in range(2):
            ex[pl.ds(2 * kind + half, shards, stride=EXTRA), :] = row[
                kind * shards : (kind + 1) * shards, half * LANES : (half + 1) * LANES
            ]
    extra_ref[...] = ex[...].astype(BF16)

    earlier = ones_where(iota((shards, shards), 1) < iota((shards, shards), 0))
    lane = iota((shards, LANES), 1)
    table_off = jnp.zeros((shards, LANES), F32)
    for g in range(groups):
        first = mark[g * span * shards : (g * span + 1) * shards, :]
        after = mark[(g + 1) * span * shards : ((g + 1) * span + 1) * shards, :]
        off = dot(earlier, (after - first).astype(BF16)) - first
        off_scr[g * shards : (g + 1) * shards, :] = off
        table_off = jnp.where(lane == g, off, table_off)
        table_off = jnp.where(lane == groups + g, after, table_off)
    off_ref[...] = table_off.astype(I32)

    total = span * count
    blocks = total // LANES
    at = iota((1, total), 1)
    sample = (at & (width - 1)).astype(F32)
    field = (at // count).astype(F32)

    def group_step(g, unused):
        owner = lanes_of(own_scr, g * span, span)
        off = off_scr[pl.ds(g * shards, shards), :]
        shifts = jnp.where(
            iota((shards, total), 0, F32) == owner,
            jnp.concatenate([off] * blocks, axis=1),
            0.0,
        )
        pos = lanes_of(rank_scr, g * span, span) + jnp.sum(shifts, axis=0, keepdims=True)
        pos = pos.astype(I32)
        block = iota((blocks, total), 0) == (pos >> 7)
        source = jnp.concatenate(
            [jnp.where(block, sample, 0.0), jnp.where(block, field, 0.0)], axis=0
        ).astype(BF16)
        col_ref[g] = dot_nt(ones_where(iota((LANES, total), 0) == (pos & 127)), source)
        return unused

    lax.fori_loop(0, groups, group_step, 0)


def request_kernel(shards, rows_dev, req_ref, place_ref, out_ref, mrow_ref, mcol_ref, table, ex):
    shift = rows_dev.bit_length() - 1
    width = req_ref.shape[1]
    rows = req_ref.shape[0]
    batch = 4
    count = batch * width
    table[...] = pack_places(place_ref[...], shift, rows_dev // shards)
    tri = strict_upper(width)
    ones = jnp.ones((width, LANES), BF16)
    lane = iota((1, count), 1)

    def step(c, carry):
        base, row, col = carry
        ids = lanes_of(req_ref, c * batch, batch)
        owner, last = look_up(table[...], ids)
        own, rank, base = rank_ids((ids >> shift).astype(F32), base, shards, tri, ones)
        at = ones_where(iota((LANES, count), 0, F32) == rank)
        field = c * (batch // 2) + lane // (2 * width)
        query = (own * (lane & (LANES - 1)).astype(F32)).astype(BF16)
        number = (own * (field + 1).astype(F32)).astype(BF16)
        high = (own * owner).astype(BF16)
        low = (own * last).astype(BF16)
        row = row + dot_nt(jnp.concatenate([high, low, query, number], axis=0), at)
        col = col + dot_nt(at, jnp.concatenate([number, number], axis=0))
        return base, row, col

    unused, row, col = lax.fori_loop(
        0,
        rows // batch,
        step,
        (
            jnp.zeros((shards, LANES), F32),
            jnp.zeros((4 * shards, LANES), F32),
            jnp.zeros((LANES, 2 * shards), F32),
        ),
    )
    ex[...] = jnp.zeros_like(ex)
    for kind in range(2):
        ex[pl.ds(kind, shards, stride=EXTRA), :] = row[kind * shards : (kind + 1) * shards]
    out_ref[...] = ex[...].astype(BF16)
    field = row[3 * shards :].astype(I32) - 1
    mrow_ref[...] = jnp.where(
        field < 0, -1, (field & 3) * LANES + row[2 * shards : 3 * shards].astype(I32)
    )
    mcol_ref[...] = jnp.where(col > 4.0, 1.0, 0.0)


def build_kernel(group, shards, off_ref, col_ref, grads_ref, extra_ref, out_ref, rows_scr):
    slots = out_ref.shape[1] - EXTRA
    samples = grads_ref.shape[0]
    groups = col_ref.shape[0]
    blocks = col_ref.shape[2] // 2
    total = blocks * LANES
    span = grads_ref.shape[1] // groups
    step = pl.program_id(0)

    @pl.when(step == 0)
    def _():
        def sort_group(g, unused):
            col = col_ref[g]
            hots = [
                ones_where(iota((LANES, samples), 1, F32) == col[:, b : b + 1])
                for b in range(blocks)
            ]
            part = grads_ref[:, pl.ds(pl.multiple_of(g * span, span), span)]
            rows = dot(jnp.concatenate(hots, axis=0), part)
            field = jnp.concatenate(
                [
                    jnp.broadcast_to(col[:, blocks + b : blocks + b + 1], (LANES, LANES))
                    for b in range(blocks)
                ],
                axis=0,
            )
            picked = rows[:, :LANES]
            for q in range(1, span // LANES):
                picked = jnp.where(field == float(q), rows[:, q * LANES : (q + 1) * LANES], picked)
            rows_scr[g, slots : slots + total, :] = picked
            return unused

        lax.fori_loop(0, groups, sort_group, 0)

    at = iota((slots, LANES), 0)

    def one(b, unused):
        owner = step * group + b
        picked = rows_scr[0, pl.ds(slots + off_ref[owner, 0], slots), :]
        for g in range(1, groups):
            start = off_ref[owner, groups + g - 1]
            rows = rows_scr[g, pl.ds(slots + off_ref[owner, g], slots), :]
            picked = jnp.where(at >= start, rows, picked)
        picked = jnp.where(at >= off_ref[owner, 2 * groups - 1], 0.0, picked)
        out_ref[b, 0:slots, :] = picked.astype(BF16)
        out_ref[b, slots : slots + EXTRA, :] = extra_ref[pl.ds(b * EXTRA, EXTRA), :]
        return unused

    lax.fori_loop(0, group, one, 0, unroll=4)


def sum_kernel(group, got_ref, extra_ref, unused_ref, out_ref, scr, hi_scr, lo_scr, total):
    shards = extra_ref.shape[0]
    slots = got_ref.shape[1] - EXTRA
    step = pl.program_id(0)

    @pl.when(step == 0)
    def _():
        scr[...] = extra_ref[...].astype(F32).reshape(scr.shape)
        lows = []
        for half in range(2):
            ranges = scr[pl.ds(half, shards, stride=EXTRA), :].astype(I32)
            within = scr[pl.ds(2 + half, shards, stride=EXTRA), :].astype(I32)
            hi_scr[half] = (ranges & 15) * 32 + within
            lows.append((ranges >> 4).astype(F32))
        lo_scr[...] = jnp.concatenate(lows, axis=0).T
        total[...] = jnp.zeros_like(total)

    turned = pltpu.roll(lo_scr[...], lax.rem(2 * shards - step * group, 2 * shards), 1)
    highs, values = [], []
    for k in range(group):
        for half in range(2):
            hi = hi_scr[half, pl.ds(step * group + k, 1), :]
            highs.append(ones_where(iota((512, LANES), 0) == hi))
            low = jnp.broadcast_to(
                turned[:, half * shards + k : half * shards + k + 1], (LANES, LANES)
            )
            rows = got_ref[k, half * LANES : (half + 1) * LANES, :]
            values.append(
                jnp.concatenate([rows * ones_where(low == float(q)) for q in range(4)], axis=1)
            )
    total[...] += dot(jnp.concatenate(highs, axis=1), jnp.concatenate(values, axis=0))

    @pl.when(step == pl.num_programs(0) - 1)
    def _():
        for q in range(4):
            out_ref[q * 512 : (q + 1) * 512, :] = total[:, q * LANES : (q + 1) * LANES]


def adagrad_kernel(table_ref, accum_ref, one_ref, two_ref, extra_ref, rows_ref, new_accum_ref, sent_ref):
    gradient = one_ref[...] + two_ref[...]
    updated = accum_ref[...] + gradient * gradient
    rows = table_ref[...] - 0.1 * gradient * lax.rsqrt(updated)
    new_accum_ref[...] = updated
    rows_ref[...] = rows
    block = sent_ref.shape[1] - EXTRA
    group = sent_ref.shape[0]
    sent_ref[:, :block, :] = rows.astype(BF16).reshape(group, block, LANES)
    sent_ref[:, block:, :] = extra_ref[...].reshape(group, EXTRA, LANES)


def widen(moved_ref):
    block = moved_ref.shape[1] - EXTRA
    quarter = moved_ref.shape[0] // 4
    return jnp.concatenate(
        [
            moved_ref[q * quarter : (q + 1) * quarter, :block, :].reshape(quarter * block, LANES)
            for q in range(4)
        ],
        axis=1,
    )


def pick_rows(count, high, low, wide):
    hots = [ones_where(iota((LANES, 512), 1, F32) == high[:, b : b + 1]) for b in range(count)]
    rows = dot(jnp.concatenate(hots, axis=0), wide)
    lows = jnp.concatenate(
        [jnp.broadcast_to(low[:, b : b + 1], (LANES, LANES)) for b in range(count)], axis=0
    )
    picked = rows[:, :LANES]
    for q in range(1, 4):
        picked = jnp.where(lows == float(q), rows[:, q * LANES : (q + 1) * LANES], picked)
    return picked.astype(BF16)


def columns_of(owner, last):
    high = ((owner & 15) * 32 + last).astype(F32)
    return jnp.concatenate([high, (owner >> 4).astype(F32)], axis=0).T


def found_kernel(group, moved_ref, out_ref, wide, cols, scr):
    shards = moved_ref.shape[0]
    step = pl.program_id(0)

    @pl.when(step == 0)
    def _():
        wide[...] = widen(moved_ref)
        block = moved_ref.shape[1] - EXTRA
        scr[...] = moved_ref[:, block:, :].astype(F32).reshape(scr.shape)
        owner = scr[pl.ds(0, shards, stride=EXTRA), :].astype(I32)
        cols[...] = columns_of(owner, scr[pl.ds(1, shards, stride=EXTRA), :].astype(I32))

    turned = pltpu.roll(cols[...], lax.rem(LANES - step * group, LANES), 1)
    picked = pick_rows(group, turned, turned[:, shards:], wide[...])
    out_ref[...] = picked.reshape(out_ref.shape)


def serving_kernel(place_ref, moved_ref, out_ref):
    place = place_ref[...]
    blocks = place.shape[0]
    zero = jnp.zeros((LANES // 2 - blocks, LANES), I32)
    cols = columns_of(
        jnp.concatenate([place >> 11, zero], axis=0), jnp.concatenate([place & 31, zero], axis=0)
    )
    out_ref[...] = pick_rows(blocks, cols, cols[:, LANES // 2 :], widen(moved_ref))


def rank_kernel(group, ret_ref, mrow_ref, mcol_ref, w_ref, b_ref, score_ref, out_ref, total):
    step = pl.program_id(0)

    @pl.when(step == 0)
    def _():
        total[...] = jnp.zeros_like(total)

    slots = ret_ref.shape[1]
    turned = pltpu.roll(mcol_ref[...], lax.rem(LANES - step * group, LANES), 1)
    hots, values = [], []
    for b in range(group):
        hots.append(
            ones_where(iota((512, slots), 0) == mrow_ref[pl.ds(step * group + b, 1), :])
        )
        low = jnp.broadcast_to(turned[:, b : b + 1], (slots, LANES))
        rows = ret_ref[b]
        values.append(
            jnp.concatenate([rows * (1.0 - low).astype(BF16), rows * low.astype(BF16)], axis=1)
        )
    total[...] += dot(jnp.concatenate(hots, axis=1), jnp.concatenate(values, axis=0))

    @pl.when(step == pl.num_programs(0) - 1)
    def _():
        pooled = jnp.concatenate(
            [
                total[(f & 3) * LANES : (f & 3) * LANES + LANES, (f >> 2) * LANES : (f >> 2) * LANES + LANES]
                for f in range(8)
            ],
            axis=1,
        ).astype(BF16)
        hidden = jnp.maximum(dot(pooled, w_ref[...]) + b_ref[...], 0.0).astype(BF16)
        out_ref[...] = dot_nt(score_ref[...], hidden)


def whole(shape):
    return pl.BlockSpec(shape, lambda *step: (0,) * len(shape))


def call(kernel, name, flops, moved, **kwargs):
    return pl.pallas_call(
        kernel,
        name=name,
        compiler_params=pltpu.CompilerParams(vmem_limit_bytes=VMEM_LIMIT),
        cost_estimate=pl.CostEstimate(flops=flops, bytes_accessed=moved, transcendentals=0),
        **kwargs,
    )


def exchange(rows):
    return lax.all_to_all(rows, "shard", split_axis=0, concat_axis=0, tiled=True)


def on_device(
    table_rows,
    accum,
    hash_keys,
    hash_place,
    sample_ids,
    sample_grads,
    req_ids,
    w_hidden,
    b_hidden,
    w_score,
):
    rows_dev, width = table_rows.shape
    shards = lax.axis_size("shard")
    samples, id_columns = sample_ids.shape
    requests = req_ids.shape[0]
    slots = 2 * samples * id_columns // shards
    req_slots = 2 * requests * id_columns // shards
    hidden_width = w_hidden.shape[1]
    per_field = id_columns * width // sample_grads.shape[1]
    block = rows_dev // shards
    groups = 4
    sorted_rows = samples * id_columns // groups
    places = hash_place.reshape(-1, LANES)
    shape = jax.ShapeDtypeStruct
    extras = shape((shards * EXTRA, LANES), BF16)
    columns = shape((LANES, 2 * shards), F32)
    table = pltpu.VMEM((2 * LANES, places.shape[0] // 2), BF16)
    ex = pltpu.VMEM(extras.shape, F32)

    col, off, extra = call(
        functools.partial(index_kernel, shards, rows_dev, per_field, groups),
        "index",
        2**33,
        2**21,
        out_shape=(
            shape((groups, LANES, 2 * sorted_rows // LANES), F32),
            shape((shards, LANES), I32),
            extras,
        ),
        scratch_shapes=[
            table,
            ex,
            pltpu.VMEM((id_columns // per_field, per_field * samples), F32),
            pltpu.VMEM((id_columns // per_field, per_field * samples), F32),
            pltpu.VMEM(((id_columns // per_field + 1) * shards, LANES), F32),
            pltpu.VMEM((groups * shards, LANES), F32),
        ],
    )(sample_ids.T, places)

    group = 16
    sent = call(
        functools.partial(build_kernel, group, shards),
        "build",
        2**33,
        2**22,
        grid=(shards // group,),
        in_specs=[
            pl.BlockSpec(memory_space=pltpu.SMEM),
            whole(col.shape),
            whole(sample_grads.shape),
            pl.BlockSpec((group * EXTRA, LANES), lambda g: (g, 0)),
        ],
        out_specs=pl.BlockSpec((group, slots + EXTRA, width), lambda g: (g, 0, 0)),
        out_shape=shape((shards, slots + EXTRA, width), BF16),
        scratch_shapes=[pltpu.VMEM((groups, sorted_rows + 2 * slots, width), F32)],
    )(off, col, sample_grads, extra)
    got = exchange(sent)

    asked, mrow, mcol = call(
        functools.partial(request_kernel, shards, rows_dev),
        "request_index",
        2**31,
        2**19,
        out_shape=(extras, shape((shards, req_slots), I32), columns),
        scratch_shapes=[table, ex],
    )(req_ids.T.reshape(-1, 2 * requests), places)

    group = 8
    partial_sum = call(
        functools.partial(sum_kernel, group),
        "gradient_sum",
        2**33,
        2**22,
        grid=(shards // group,),
        in_specs=[
            pl.BlockSpec((group, slots + EXTRA, width), lambda g: (g, 0, 0)),
            pl.BlockSpec((shards, EXTRA, width), lambda g: (0, slots // EXTRA, 0)),
            pl.BlockSpec(memory_space=pl.ANY),
        ],
        out_specs=whole((rows_dev, width)),
        out_shape=shape((rows_dev, width), F32),
        scratch_shapes=[
            ex,
            pltpu.VMEM((2, shards, LANES), I32),
            pltpu.VMEM((LANES, LANES), F32),
            pltpu.VMEM((512, 512), F32),
        ],
    )(got, got, mrow)
    other = lax.ppermute(partial_sum, "rep", [(0, 1), (1, 0)])

    steps = 4
    rows_spec = pl.BlockSpec((rows_dev // steps, width), lambda g: (g, 0))
    new_rows, new_accum, moved = call(
        adagrad_kernel,
        "adagrad",
        2**21,
        2**23,
        grid=(steps,),
        in_specs=[rows_spec] * 4
        + [pl.BlockSpec((shards * EXTRA // steps, LANES), lambda g: (g, 0))],
        out_specs=(
            rows_spec,
            rows_spec,
            pl.BlockSpec((shards // steps, block + EXTRA, width), lambda g: (g, 0, 0)),
        ),
        out_shape=(
            shape((rows_dev, width), F32),
            shape((rows_dev, width), F32),
            shape((shards, block + EXTRA, width), BF16),
        ),
    )(table_rows, accum, partial_sum, other, asked)
    moved = exchange(moved)

    group = 16
    found = call(
        functools.partial(found_kernel, group),
        "found",
        2**32,
        2**22,
        grid=(shards // group,),
        in_specs=[whole(moved.shape)],
        out_specs=pl.BlockSpec((group, req_slots, width), lambda g: (g, 0, 0)),
        out_shape=shape((shards, req_slots, width), BF16),
        scratch_shapes=[
            pltpu.VMEM((512, 512), BF16),
            pltpu.VMEM((LANES, LANES), F32),
            ex,
        ],
    )(moved)
    returned = exchange(found)

    place_rows = rows_dev // LANES
    own_places = lax.dynamic_slice_in_dim(
        places, lax.axis_index("shard") * place_rows, place_rows, axis=0
    )
    serving_rows = call(
        serving_kernel,
        "serving",
        2**30,
        2**20,
        out_shape=shape((rows_dev, width), BF16),
    )(own_places, moved)

    scores = call(
        functools.partial(rank_kernel, group),
        "pool_rank",
        2**32,
        2**22,
        grid=(shards // group,),
        in_specs=[
            pl.BlockSpec((group, req_slots, width), lambda g: (g, 0, 0)),
            whole((shards, req_slots)),
            whole(columns.shape),
            whole(w_hidden.shape),
            whole((1, hidden_width)),
            whole((1, hidden_width)),
        ],
        out_specs=whole((1, requests)),
        out_shape=shape((1, requests), F32),
        scratch_shapes=[pltpu.VMEM((512, 256), F32)],
    )(returned, mrow, mcol, w_hidden, b_hidden.reshape(1, -1), w_score.reshape(1, -1))
    return (new_rows, new_accum, serving_rows, scores.reshape(requests))


def solution(mesh):
    return jax.shard_map(
        on_device,
        mesh=mesh,
        in_specs=(
            P("shard", None),
            P("shard", None),
            P("shard"),
            P(),
            P(("rep", "shard"), None),
            P(("rep", "shard"), None),
            P(("rep", "shard"), None),
            P(),
            P(),
            P(),
        ),
        out_specs=(P("shard", None), P("shard", None), P("shard", None), P(("rep", "shard"))),
        check_vma=False,
    )
```

time: 234 us -> 190 us (0.81)
  Pallas kernels: 104 us -> 63.3 us
  blocking collectives: 67.1 us -> 28.7 us
  waiting for transfers between devices: 43 us -> 75 us
  starting transfers between devices: 10.1 us -> 16.9 us
  other arithmetic: 3 us -> 0 us
    pallas_call x5 -> x8, Pallas kernels: 104 us -> 63.3 us  [the longest x1 15.3 us: on_device(): call(functools.partial(sum_kernel, group), 'gradient_sum', 2 ** 33, 2 **...]
    all_to_all x1, blocking collectives: 67.1 us -> 28.7 us  [exchange(): lax.all_to_all(rows, 'shard', split_axis=0, concat_axis=0, tiled=True)]
    all_to_all x2, waiting for transfers between devices: 40.2 us -> 72.2 us  [exchange(): lax.all_to_all(rows, 'shard', split_axis=0, concat_axis=0, tiled=True)]
    all_to_all x2, starting transfers between devices: 10.1 us -> 16.9 us  [exchange(): lax.all_to_all(rows, 'shard', split_axis=0, concat_axis=0, tiled=True)]
    convert_element_type x1 -> x0, other arithmetic: 3 us -> none  [on_device(): new_rows.astype(BF16).reshape(shards, rows_dev // shards, row_width)]
  transfers between devices with their start and end apart: 3 -> 3, of which waited for: 3 -> 3; matrix products, arithmetic and copies ran while one was open for 1% -> 1% of each run, Pallas kernels for 0% -> 5%
where the time goes in v1:
time: 190 us; the launch traced here: 189 us
  waiting for transfers between devices  75 us (39%)
  Pallas kernels  63.3 us (33%)
  blocking collectives  28.7 us (15%)
  starting transfers between devices  16.9 us (9%)
  local copies, waits for them, and re-layouts  4.8 us (3%)
    all_to_all x2, waiting for transfers between devices, exchange(): lax.all_to_all(rows, 'shard', split_axis=0, concat_axis=0, tiled=True)  72.2 us
    all_to_all x1, blocking collectives, exchange(): lax.all_to_all(rows, 'shard', split_axis=0, concat_axis=0, tiled=True)  28.7 us
    all_to_all x2, starting transfers between devices, exchange(): lax.all_to_all(rows, 'shard', split_axis=0, concat_axis=0, tiled=True)  16.9 us
    pallas_call x1, Pallas kernels, on_device(): call(functools.partial(sum_kernel, group), 'gradient_sum', 2 ** 33, 2 **...  15.3 us
    pallas_call x1, Pallas kernels, on_device(): call(functools.partial(index_kernel, shards, rows_dev, per_field, groups)...  11.2 us
    pallas_call x1, Pallas kernels, on_device(): call(functools.partial(build_kernel, group, shards), 'build', 2 ** 33, 2...  8.69 us
    pallas_call x1, Pallas kernels, on_device(): call(functools.partial(found_kernel, group), 'found', 2 ** 32, 2 ** 22, g...  7.68 us
    pallas_call x1, Pallas kernels, on_device(): call(functools.partial(rank_kernel, group), 'pool_rank', 2 ** 32, 2 ** 22...  7.04 us
  transfers between devices with their start and end apart: 3, of which 3 were waited for; matrix products, arithmetic and copies ran while one was open for 1% of the time, Pallas kernels for 5%

profile of v1, /device:TPU:0, one launch (start us, length us, event | category | flops | bytes accessed | tf_op | source)
XLA Modules:
  0.0 189.4 jit_solution(10455509591572929169)
XLA Ops:
  0.6 11.2 %index.1 = (f32[4,128,32]{2,1,0:T(8,128)}, s32[64,128]{1,0:T(8,128)}, bf16[1024,128]{1,0:T(8,128)(2,1)}) custom-call(s32[32,256]{1,0:T(8,128)} %bitcast.9, s32[1024,128]{1,0:T(8,128)} %bitcast.6), custom_call_target="tpu_custom_call" | custom-call | flops 8589934592 | bytes 2097152 | tf_op jit(solution)/shard_map/index/pallas_call | solution.py:448
  11.9 8.7 %build.1 = bf16[64,272,128]{2,1,0:T(8,128)(2,1)} custom-call(s32[64,128]{1,0:T(8,128)} %get-tuple-element.13.off_ref, f32[4,128,32]{2,1,0:T(8,128)} %get-tuple-element.14.col_ref, bf16[256,1024]{1,0:T(8,128)(2,1)} %grads_ref.1, bf16[1024,128]{1,0:T(8,128)(2,1)} %get-tuple-element.15.extra_ref), custom_call_target="tpu_custom_call" | custom-call | flops 8589934592 | bytes 4194304 | tf_op jit(solution)/shard_map/build/pallas_call | solution.py:469
  20.6 0.0 copy-start.2
  20.6 11.9 %all-to-all-start = ((bf16[64,272,128]{2,1,0:T(8,128)(2,1)}), bf16[64,272,128]{2,1,0:T(8,128)(2,1)}, u32[]{:S(2)}, u32[]{:S(2)}) async-start(bf16[64,272,128]{2,1,0:T(8,128)(2,1)} %build.1), calls=%async_computation | async-start | bytes 8912896 | tf_op jit(solution)/shard_map/all_to_all | solution.py:415
  32.4 0.0 copy-done.2
  32.4 0.6 reshape.24.req_ref
  33.0 5.7 %request_index.1 = (bf16[1024,128]{1,0:T(8,128)(2,1)}, s32[64,128]{1,0:T(8,128)}, f32[128,128]{1,0:T(8,128)}) custom-call(s32[16,256]{1,0:T(8,128)} %reshape.24.req_ref, s32[1024,128]{1,0:T(8,128)} %bitcast.7), custom_call_target="tpu_custom_call" | custom-call | flops 2147483648 | bytes 524288 | tf_op jit(solution)/shard_map/request_index/pallas_call | solution.py:487
  38.8 49.0 %all-to-all-done.got_ref.extra_ref = bf16[64,272,128]{2,1,0:T(8,128)(2,1)} async-done(((bf16[64,272,128]{2,1,0:T(8,128)(2,1)}), bf16[64,272,128]{2,1,0:T(8,128)(2,1)}, u32[]{:S(2)}, u32[]{:S(2)}) %all-to-all-start) | async-done | bytes 4456480 | tf_op jit(solution)/shard_map/all_to_all | solution.py:415
  87.8 15.3 %gradient_sum.1.one_ref = f32[2048,128]{1,0:T(8,128)} custom-call(bf16[64,272,128]{2,1,0:T(8,128)(2,1)} %all-to-all-done.got_ref.extra_ref, bf16[64,272,128]{2,1,0:T(8,128)(2,1)} %all-to-all-done.got_ref.extra_ref, s32[64,128]{1,0:T(8,128)} %get-tuple-element.16.unused_ref.mrow_ref), custom_call_target="tpu_custom_call" | custom-call | flops 8589934592 | bytes 4194304 | tf_op jit(solution)/shard_map/gradient_sum/pallas_call | solution.py:497
  103.1 0.0 collective-permute-start
  103.1 2.9 %collective-permute-done.two_ref = f32[2048,128]{1,0:T(8,128)S(1)} collective-permute-done((f32[2048,128]{1,0:T(8,128)}, f32[2048,128]{1,0:T(8,128)S(1)}, u32[]{:S(2)}, u32[]{:S(2)}) %collective-permute-start) | collective-permute-done | bytes 1048608 | tf_op jit(solution)/shard_map/ppermute | solution.py:517
  105.9 0.0 copy-start.1
  105.9 1.0 copy-done.1
  106.9 4.3 %adagrad.1 = (f32[2048,128]{1,0:T(8,128)}, f32[2048,128]{1,0:T(8,128)}, bf16[64,48,128]{2,1,0:T(8,128)(2,1)}) custom-call(f32[2048,128]{1,0:T(8,128)} %table_ref.1, f32[2048,128]{1,0:T(8,128)} %accum_ref.1, f32[2048,128]{1,0:T(8,128)} %gradient_sum.1.one_ref, f32[2048,128]{1,0:T(8,128)} %copy-done.1, bf16[1024,128]{1,0:T(8,128)(2,1)} %get-tuple-element.17.extra_ref), custom_call_target="tpu_custom_call" | custom-call | flops 2097152 | bytes 8388608 | tf_op jit(solution)/shard_map/adagrad/pallas_call | solution.py:521
  111.2 28.7 %all_to_all.15.moved_ref = bf16[64,48,128]{2,1,0:T(8,128)(2,1)} all-to-all(bf16[64,48,128]{2,1,0:T(8,128)(2,1)} %get-tuple-element.20), channel_id=1, replica_groups=mesh['rep'=2,'shard'=64] {'shard'}, dimensions={0} | all-to-all | bytes 1572864 | tf_op jit(solution)/shard_map/all_to_all | solution.py:415
  139.9 7.7 %found.1 = bf16[64,128,128]{2,1,0:T(8,128)(2,1)} custom-call(bf16[64,48,128]{2,1,0:T(8,128)(2,1)} %all_to_all.15.moved_ref), custom_call_target="tpu_custom_call" | custom-call | flops 4294967296 | bytes 4194304 | tf_op jit(solution)/shard_map/found/pallas_call | solution.py:543
  147.6 0.0 copy-start.3
  147.6 5.1 %all-to-all-start.2 = ((bf16[64,128,128]{2,1,0:T(8,128)(2,1)}), bf16[64,128,128]{2,1,0:T(8,128)(2,1)S(1)}, u32[]{:S(2)}, u32[]{:S(2)}) async-start(bf16[64,128,128]{2,1,0:T(8,128)(2,1)} %found.1), calls=%async_computation.2 | async-start | bytes 4194304 | tf_op jit(solution)/shard_map/all_to_all | solution.py:415
  152.6 0.0 copy-done.3
  152.7 0.6 reshape.26.score_ref
  153.3 1.3 constant_dynamic-slice_fusion.place_ref
  154.5 3.3 %serving.1 = bf16[2048,128]{1,0:T(8,128)(2,1)} custom-call(s32[16,128]{1,0:T(8,128)} %constant_dynamic-slice_fusion.place_ref, bf16[64,48,128]{2,1,0:T(8,128)(2,1)} %all_to_all.15.moved_ref), custom_call_target="tpu_custom_call" | custom-call | flops 1073741824 | bytes 1048576 | tf_op jit(solution)/shard_map/serving/pallas_call | solution.py:564
  157.9 23.2 %all-to-all-done.2.ret_ref = bf16[64,128,128]{2,1,0:T(8,128)(2,1)S(1)} async-done(((bf16[64,128,128]{2,1,0:T(8,128)(2,1)}), bf16[64,128,128]{2,1,0:T(8,128)(2,1)S(1)}, u32[]{:S(2)}, u32[]{:S(2)}) %all-to-all-start.2) | async-done | bytes 2097184 | tf_op jit(solution)/shard_map/all_to_all | solution.py:415
  181.1 0.0 copy-start
  181.1 1.3 copy-done
  182.4 7.0 %pool_rank.1 = f32[1,128]{1,0:T(1,128)} custom-call(bf16[64,128,128]{2,1,0:T(8,128)(2,1)} %copy-done, s32[64,128]{1,0:T(8,128)} %get-tuple-element.16.unused_ref.mrow_ref, f32[128,128]{1,0:T(8,128)} %get-tuple-element.21.mcol_ref, bf16[1024,1024]{1,0:T(8,128)(2,1)} %w_ref.1, f32[1,1024]{1,0:T(1,128)} %bitcast.10, bf16[1,1024]{1,0:T(2,128)(2,1)} %reshape.26.score_ref), custom_call_target="tpu_custom_call" | custom-call | flops 4294967296 | bytes 4194304 | tf_op jit(solution)/shard_map/pool_rank/pallas_call | solution.py:572
Async XLA Ops:
  20.6 11.9 %copy-start.2 = (s32[128,32]{0,1:T(8,128)S(1)}, s32[128,32]{0,1:T(8,128)}, u32[]{:S(2)}) copy-start(s32[128,32]{0,1:T(8,128)} %param.15) | copy-start | bytes 49156
  20.6 67.2 %all-to-all-start = ((bf16[64,272,128]{2,1,0:T(8,128)(2,1)}), bf16[64,272,128]{2,1,0:T(8,128)(2,1)}, u32[]{:S(2)}, u32[]{:S(2)}) async-start(bf16[64,272,128]{2,1,0:T(8,128)(2,1)} %build.1), calls=%async_computation | async-start | bytes 8912896 | tf_op jit(solution)/shard_map/all_to_all | solution.py:415
  103.1 2.9 %collective-permute-start = (f32[2048,128]{1,0:T(8,128)}, f32[2048,128]{1,0:T(8,128)S(1)}, u32[]{:S(2)}, u32[]{:S(2)}) collective-permute-start(f32[2048,128]{1,0:T(8,128)} %gradient_sum.1.one_ref), channel_id=1, source_target_pairs={{0,64},{64,0},{1,65},{65,1},{2,66},{66,2},{3,67},{67,3},{4,68},{68... | collective-permute-start | bytes 3145736 | tf_op jit(solution)/shard_map/ppermute | solution.py:517
  105.9 1.0 copy-start.1
  147.6 5.1 %copy-start.3 = (bf16[1024]{0:T(1024)(128)(2,1)S(1)}, bf16[1024]{0:T(1024)(128)(2,1)}, u32[]{:S(2)}) copy-start(bf16[1024]{0:T(1024)(128)(2,1)} %param.18) | copy-start | bytes 6148
  147.6 33.5 %all-to-all-start.2 = ((bf16[64,128,128]{2,1,0:T(8,128)(2,1)}), bf16[64,128,128]{2,1,0:T(8,128)(2,1)S(1)}, u32[]{:S(2)}, u32[]{:S(2)}) async-start(bf16[64,128,128]{2,1,0:T(8,128)(2,1)} %found.1), calls=%async_computation.2 | async-start | bytes 4194304 | tf_op jit(solution)/shard_map/all_to_all | solution.py:415
  181.1 1.3 copy-start

commit v2 on v1

--- a/solution.py
+++ b/solution.py
@@ -9,9 +9,10 @@
 
 F32, BF16, I32 = jnp.float32, jnp.bfloat16, jnp.int32
 NT = (((1,), (1,)), ((), ()))
-VMEM_LIMIT = 60 * 2**20
+SMALL, LARGE = 32 * 2**20, 60 * 2**20
 EXTRA = 16
 LANES = 128
+REQ_SLOTS = 112
 
 
 def iota(shape, axis, dtype=I32):
@@ -82,7 +83,8 @@
 
 def index_kernel(
     shards, rows_dev, per_field, groups,
-    ids_ref, place_ref, col_ref, off_ref, extra_ref, table, ex, own_scr, rank_scr, mark, off_scr,
+    ids_ref, place_ref, req_ref, col_ref, off_ref, extra_ref, mrow_ref, mcol_ref,
+    table, ex, own_scr, rank_scr, mark, off_scr,
 ):
     shift = rows_dev.bit_length() - 1
     width = ids_ref.shape[1]
@@ -119,6 +121,7 @@
             ex[pl.ds(2 * kind + half, shards, stride=EXTRA), :] = row[
                 kind * shards : (kind + 1) * shards, half * LANES : (half + 1) * LANES
             ]
+    index_requests(shards, shift, req_ref, table, ex, mrow_ref, mcol_ref)
     extra_ref[...] = ex[...].astype(BF16)
 
     earlier = ones_where(iota((shards, shards), 1) < iota((shards, shards), 0))
@@ -159,13 +162,10 @@
     lax.fori_loop(0, groups, group_step, 0)
 
 
-def request_kernel(shards, rows_dev, req_ref, place_ref, out_ref, mrow_ref, mcol_ref, table, ex):
-    shift = rows_dev.bit_length() - 1
+def index_requests(shards, shift, req_ref, table, ex, mrow_ref, mcol_ref):
     width = req_ref.shape[1]
-    rows = req_ref.shape[0]
     batch = 4
     count = batch * width
-    table[...] = pack_places(place_ref[...], shift, rows_dev // shards)
     tri = strict_upper(width)
     ones = jnp.ones((width, LANES), BF16)
     lane = iota((1, count), 1)
@@ -174,20 +174,20 @@
         base, row, col = carry
         ids = lanes_of(req_ref, c * batch, batch)
         owner, last = look_up(table[...], ids)
-        own, rank, base = rank_ids((ids >> shift).astype(F32), base, shards, tri, ones)
-        at = ones_where(iota((LANES, count), 0, F32) == rank)
+        own, rank, base = rank_ids(owner, base, shards, tri, ones)
+        at = ones_where(iota((LANES, count), 0, F32) == jnp.where(rank < REQ_SLOTS, rank, -1.0))
         field = c * (batch // 2) + lane // (2 * width)
         query = (own * (lane & (LANES - 1)).astype(F32)).astype(BF16)
         number = (own * (field + 1).astype(F32)).astype(BF16)
-        high = (own * owner).astype(BF16)
+        high = (own * (ids >> shift).astype(F32)).astype(BF16)
         low = (own * last).astype(BF16)
         row = row + dot_nt(jnp.concatenate([high, low, query, number], axis=0), at)
         col = col + dot_nt(at, jnp.concatenate([number, number], axis=0))
         return base, row, col
 
-    unused, row, col = lax.fori_loop(
+    base, row, col = lax.fori_loop(
         0,
-        rows // batch,
+        req_ref.shape[0] // batch,
         step,
         (
             jnp.zeros((shards, LANES), F32),
@@ -195,10 +195,10 @@
             jnp.zeros((LANES, 2 * shards), F32),
         ),
     )
-    ex[...] = jnp.zeros_like(ex)
-    for kind in range(2):
-        ex[pl.ds(kind, shards, stride=EXTRA), :] = row[kind * shards : (kind + 1) * shards]
-    out_ref[...] = ex[...].astype(BF16)
+    most = jnp.broadcast_to(jnp.max(base, axis=0, keepdims=True), (shards, LANES)).astype(I32)
+    parts = [row[:shards], row[shards : 2 * shards], (most >> 5).astype(F32), (most & 31).astype(F32)]
+    for kind, part in enumerate(parts):
+        ex[pl.ds(4 + kind, shards, stride=EXTRA), :] = part
     field = row[3 * shards :].astype(I32) - 1
     mrow_ref[...] = jnp.where(
         field < 0, -1, (field & 3) * LANES + row[2 * shards : 3 * shards].astype(I32)
@@ -257,7 +257,7 @@
     lax.fori_loop(0, group, one, 0, unroll=4)
 
 
-def sum_kernel(group, got_ref, extra_ref, unused_ref, out_ref, scr, hi_scr, lo_scr, total):
+def sum_kernel(group, got_ref, extra_ref, out_ref, picks_ref, scr, hi_scr, lo_scr, total):
     shards = extra_ref.shape[0]
     slots = got_ref.shape[1] - EXTRA
     step = pl.program_id(0)
@@ -273,6 +273,11 @@
             lows.append((ranges >> 4).astype(F32))
         lo_scr[...] = jnp.concatenate(lows, axis=0).T
         total[...] = jnp.zeros_like(total)
+        kinds = [scr[pl.ds(kind, shards, stride=EXTRA), :].astype(I32) for kind in range(4, 8)]
+        high = (kinds[0] & 15) * 32 + kinds[1]
+        picks_ref[...] = jnp.concatenate([high, kinds[0] >> 4], axis=0).astype(F32).T
+        most = jnp.max((kinds[2] * 32 + kinds[3]).astype(F32), axis=0, keepdims=True)
+        out_ref[4 * 512 :, :] = jnp.broadcast_to(most, (8, LANES))
 
     turned = pltpu.roll(lo_scr[...], lax.rem(2 * shards - step * group, 2 * shards), 1)
     highs, values = [], []
@@ -295,35 +300,13 @@
             out_ref[q * 512 : (q + 1) * 512, :] = total[:, q * LANES : (q + 1) * LANES]
 
 
-def adagrad_kernel(table_ref, accum_ref, one_ref, two_ref, extra_ref, rows_ref, new_accum_ref, sent_ref):
-    gradient = one_ref[...] + two_ref[...]
-    updated = accum_ref[...] + gradient * gradient
-    rows = table_ref[...] - 0.1 * gradient * lax.rsqrt(updated)
-    new_accum_ref[...] = updated
-    rows_ref[...] = rows
-    block = sent_ref.shape[1] - EXTRA
-    group = sent_ref.shape[0]
-    sent_ref[:, :block, :] = rows.astype(BF16).reshape(group, block, LANES)
-    sent_ref[:, block:, :] = extra_ref[...].reshape(group, EXTRA, LANES)
-
-
-def widen(moved_ref):
-    block = moved_ref.shape[1] - EXTRA
-    quarter = moved_ref.shape[0] // 4
-    return jnp.concatenate(
-        [
-            moved_ref[q * quarter : (q + 1) * quarter, :block, :].reshape(quarter * block, LANES)
-            for q in range(4)
-        ],
-        axis=1,
-    )
-
-
-def pick_rows(count, high, low, wide):
-    hots = [ones_where(iota((LANES, 512), 1, F32) == high[:, b : b + 1]) for b in range(count)]
+def pick_rows(count, height, high, low, wide):
+    hots = [
+        ones_where(iota((height, 512), 1, F32) == high[:height, b : b + 1]) for b in range(count)
+    ]
     rows = dot(jnp.concatenate(hots, axis=0), wide)
     lows = jnp.concatenate(
-        [jnp.broadcast_to(low[:, b : b + 1], (LANES, LANES)) for b in range(count)], axis=0
+        [jnp.broadcast_to(low[:height, b : b + 1], (height, LANES)) for b in range(count)], axis=0
     )
     picked = rows[:, :LANES]
     for q in range(1, 4):
@@ -331,58 +314,67 @@
     return picked.astype(BF16)
 
 
-def columns_of(owner, last):
-    high = ((owner & 15) * 32 + last).astype(F32)
-    return jnp.concatenate([high, (owner >> 4).astype(F32)], axis=0).T
-
-
-def found_kernel(group, moved_ref, out_ref, wide, cols, scr):
-    shards = moved_ref.shape[0]
+def update_kernel(
+    group, table_ref, accum_ref, one_ref, two_ref, picks_ref, rows_ref, accum_out_ref, sent_ref,
+    most_ref, rows, updated, moved, wide, sems,
+):
     step = pl.program_id(0)
+    count = rows.shape[0]
+    copies = (
+        pltpu.make_async_copy(rows, rows_ref, sems.at[0]),
+        pltpu.make_async_copy(updated, accum_out_ref, sems.at[1]),
+    )
 
     @pl.when(step == 0)
     def _():
-        wide[...] = widen(moved_ref)
-        block = moved_ref.shape[1] - EXTRA
-        scr[...] = moved_ref[:, block:, :].astype(F32).reshape(scr.shape)
-        owner = scr[pl.ds(0, shards, stride=EXTRA), :].astype(I32)
-        cols[...] = columns_of(owner, scr[pl.ds(1, shards, stride=EXTRA), :].astype(I32))
-
-    turned = pltpu.roll(cols[...], lax.rem(LANES - step * group, LANES), 1)
-    picked = pick_rows(group, turned, turned[:, shards:], wide[...])
-    out_ref[...] = picked.reshape(out_ref.shape)
-
-
-def serving_kernel(place_ref, moved_ref, out_ref):
-    place = place_ref[...]
-    blocks = place.shape[0]
-    zero = jnp.zeros((LANES // 2 - blocks, LANES), I32)
-    cols = columns_of(
-        jnp.concatenate([place >> 11, zero], axis=0), jnp.concatenate([place & 31, zero], axis=0)
-    )
-    out_ref[...] = pick_rows(blocks, cols, cols[:, LANES // 2 :], widen(moved_ref))
-
-
-def rank_kernel(group, ret_ref, mrow_ref, mcol_ref, w_ref, b_ref, score_ref, out_ref, total):
+        most_ref[...] = jnp.maximum(one_ref[count:, :], two_ref[count:, :])
+        gradient = one_ref[:count, :] + two_ref[:count, :]
+        history = accum_ref[...] + gradient * gradient
+        updated[...] = history
+        rows[...] = table_ref[...] - 0.1 * gradient * lax.rsqrt(history)
+        for copy in copies:
+            copy.start()
+        moved[...] = rows[...].astype(BF16)
+        wide[...] = jnp.concatenate(
+            [moved[q * 512 : (q + 1) * 512, :] for q in range(4)], axis=1
+        )
+
+    turned = pltpu.roll(picks_ref[...], lax.rem(LANES - step * group, LANES), 1)
+    picked = pick_rows(group, REQ_SLOTS, turned, turned[:, LANES // 2 :], wide[...])
+    sent_ref[:, :REQ_SLOTS, :] = picked.reshape(group, REQ_SLOTS, LANES)
+    block = sent_ref.shape[1] - REQ_SLOTS
+    start = pl.multiple_of(step * (group * block), group * block)
+    sent_ref[:, REQ_SLOTS:, :] = moved[pl.ds(start, group * block), :].reshape(group, block, LANES)
+
+    @pl.when(step == pl.num_programs(0) - 1)
+    def _():
+        for copy in copies:
+            copy.wait()
+
+
+def rank_kernel(
+    group, ret_ref, mrow_ref, mcol_ref, place_ref, w_ref, b_ref, score_ref, out_ref, serving_ref,
+    total, wide,
+):
     step = pl.program_id(0)
 
     @pl.when(step == 0)
     def _():
         total[...] = jnp.zeros_like(total)
 
-    slots = ret_ref.shape[1]
     turned = pltpu.roll(mcol_ref[...], lax.rem(LANES - step * group, LANES), 1)
     hots, values = [], []
     for b in range(group):
         hots.append(
-            ones_where(iota((512, slots), 0) == mrow_ref[pl.ds(step * group + b, 1), :])
+            ones_where(iota((512, LANES), 0) == mrow_ref[pl.ds(step * group + b, 1), :])
         )
-        low = jnp.broadcast_to(turned[:, b : b + 1], (slots, LANES))
-        rows = ret_ref[b]
+        low = jnp.broadcast_to(turned[:, b : b + 1], (LANES, LANES))
+        rows = ret_ref[b, :LANES, :]
         values.append(
             jnp.concatenate([rows * (1.0 - low).astype(BF16), rows * low.astype(BF16)], axis=1)
         )
     total[...] += dot(jnp.concatenate(hots, axis=1), jnp.concatenate(values, axis=0))
+    wide[step] = ret_ref[:, REQ_SLOTS:, :].reshape(wide.shape[1:])
 
     @pl.when(step == pl.num_programs(0) - 1)
     def _():
@@ -395,17 +387,49 @@
         ).astype(BF16)
         hidden = jnp.maximum(dot(pooled, w_ref[...]) + b_ref[...], 0.0).astype(BF16)
         out_ref[...] = dot_nt(score_ref[...], hidden)
+        place = place_ref[...]
+        owner, last = place >> 11, place & 31
+        high = ((owner & 15) * 32 + last).astype(F32)
+        zero = jnp.zeros((LANES // 2 - place.shape[0], LANES), F32)
+        cols = jnp.concatenate([high, zero, (owner >> 4).astype(F32), zero], axis=0).T
+        moved = jnp.concatenate([wide[q] for q in range(4)], axis=1)
+        serving_ref[...] = pick_rows(
+            place.shape[0], LANES, cols, cols[:, LANES // 2 :], moved
+        )
+
+
+def bucket_slots(targets, target_count, capacity):
+    one_hot = (targets[:, None] == jnp.arange(target_count, dtype=I32)[None, :]).astype(I32)
+    ranking = jnp.sum(jnp.cumsum(one_hot, axis=0) * one_hot, axis=1) - 1
+    return targets * capacity + ranking
+
+
+def range_scores(serving_rows, req_ids, w_hidden, b_hidden, w_score, shards, fields):
+    rows_dev, width = serving_rows.shape
+    requests, id_columns = req_ids.shape
+    capacity = 2 * requests * id_columns // shards
+    flat = req_ids.reshape(-1)
+    slot = bucket_slots(flat // rows_dev, shards, capacity)
+    keys = jnp.zeros((shards * capacity,), I32).at[slot].set(flat % rows_dev)
+    asked = exchange(keys.reshape(shards, capacity))
+    found = jnp.take(serving_rows, asked.reshape(-1), axis=0, mode="clip")
+    returned = exchange(found.reshape(shards, capacity, width)).reshape(-1, width)
+    rows = jnp.take(returned, slot, axis=0, mode="clip").astype(F32)
+    pooled = jnp.sum(rows.reshape(requests * fields, id_columns // fields, width), axis=1)
+    pooled = pooled.astype(BF16).reshape(requests, fields * width)
+    hidden = jnp.dot(pooled, w_hidden, preferred_element_type=F32) + b_hidden
+    return jnp.dot(jax.nn.relu(hidden).astype(BF16), w_score, preferred_element_type=F32)
 
 
 def whole(shape):
     return pl.BlockSpec(shape, lambda *step: (0,) * len(shape))
 
 
-def call(kernel, name, flops, moved, **kwargs):
+def call(kernel, name, flops, moved, limit=SMALL, **kwargs):
     return pl.pallas_call(
         kernel,
         name=name,
-        compiler_params=pltpu.CompilerParams(vmem_limit_bytes=VMEM_LIMIT),
+        compiler_params=pltpu.CompilerParams(vmem_limit_bytes=limit),
         cost_estimate=pl.CostEstimate(flops=flops, bytes_accessed=moved, transcendentals=0),
         **kwargs,
     )
@@ -432,7 +456,6 @@
     samples, id_columns = sample_ids.shape
     requests = req_ids.shape[0]
     slots = 2 * samples * id_columns // shards
-    req_slots = 2 * requests * id_columns // shards
     hidden_width = w_hidden.shape[1]
     per_field = id_columns * width // sample_grads.shape[1]
     block = rows_dev // shards
@@ -445,15 +468,18 @@
     table = pltpu.VMEM((2 * LANES, places.shape[0] // 2), BF16)
     ex = pltpu.VMEM(extras.shape, F32)
 
-    col, off, extra = call(
+    col, off, extra, mrow, mcol = call(
         functools.partial(index_kernel, shards, rows_dev, per_field, groups),
         "index",
         2**33,
         2**21,
+        LARGE,
         out_shape=(
             shape((groups, LANES, 2 * sorted_rows // LANES), F32),
             shape((shards, LANES), I32),
             extras,
+            shape((shards, LANES), I32),
+            columns,
         ),
         scratch_shapes=[
             table,
@@ -463,7 +489,7 @@
             pltpu.VMEM(((id_columns // per_field + 1) * shards, LANES), F32),
             pltpu.VMEM((groups * shards, LANES), F32),
         ],
-    )(sample_ids.T, places)
+    )(sample_ids.T, places, req_ids.T.reshape(-1, 2 * requests))
 
     group = 16
     sent = call(
@@ -471,6 +497,7 @@
         "build",
         2**33,
         2**22,
+        LARGE,
         grid=(shards // group,),
         in_specs=[
             pl.BlockSpec(memory_space=pltpu.SMEM),
@@ -484,17 +511,8 @@
     )(off, col, sample_grads, extra)
     got = exchange(sent)
 
-    asked, mrow, mcol = call(
-        functools.partial(request_kernel, shards, rows_dev),
-        "request_index",
-        2**31,
-        2**19,
-        out_shape=(extras, shape((shards, req_slots), I32), columns),
-        scratch_shapes=[table, ex],
-    )(req_ids.T.reshape(-1, 2 * requests), places)
-
     group = 8
-    partial_sum = call(
+    partial_sum, picks = call(
         functools.partial(sum_kernel, group),
         "gradient_sum",
         2**33,
@@ -503,91 +521,87 @@
         in_specs=[
             pl.BlockSpec((group, slots + EXTRA, width), lambda g: (g, 0, 0)),
             pl.BlockSpec((shards, EXTRA, width), lambda g: (0, slots // EXTRA, 0)),
-            pl.BlockSpec(memory_space=pl.ANY),
         ],
-        out_specs=whole((rows_dev, width)),
-        out_shape=shape((rows_dev, width), F32),
+        out_specs=(whole((rows_dev + 8, width)), whole(columns.shape)),
+        out_shape=(shape((rows_dev + 8, width), F32), columns),
         scratch_shapes=[
             ex,
             pltpu.VMEM((2, shards, LANES), I32),
             pltpu.VMEM((LANES, LANES), F32),
             pltpu.VMEM((512, 512), F32),
         ],
-    )(got, got, mrow)
+    )(got, got)
     other = lax.ppermute(partial_sum, "rep", [(0, 1), (1, 0)])
 
-    steps = 4
-    rows_spec = pl.BlockSpec((rows_dev // steps, width), lambda g: (g, 0))
-    new_rows, new_accum, moved = call(
-        adagrad_kernel,
-        "adagrad",
-        2**21,
+    group = 16
+    rows_type = shape((rows_dev, width), F32)
+    any_space = pl.BlockSpec(memory_space=pl.ANY)
+    new_rows, new_accum, sent, most = call(
+        functools.partial(update_kernel, group),
+        "update",
+        2**32,
         2**23,
-        grid=(steps,),
-        in_specs=[rows_spec] * 4
-        + [pl.BlockSpec((shards * EXTRA // steps, LANES), lambda g: (g, 0))],
+        grid=(shards // group,),
+        in_specs=[
+            whole(table_rows.shape),
+            whole(accum.shape),
+            whole(partial_sum.shape),
+            whole(partial_sum.shape),
+            whole(columns.shape),
+        ],
         out_specs=(
-            rows_spec,
-            rows_spec,
-            pl.BlockSpec((shards // steps, block + EXTRA, width), lambda g: (g, 0, 0)),
+            any_space,
+            any_space,
+            pl.BlockSpec((group, REQ_SLOTS + block, width), lambda g: (g, 0, 0)),
+            whole((8, LANES)),
         ),
         out_shape=(
-            shape((rows_dev, width), F32),
-            shape((rows_dev, width), F32),
-            shape((shards, block + EXTRA, width), BF16),
+            rows_type,
+            rows_type,
+            pltpu.HBM((shards, REQ_SLOTS + block, width), BF16),
+            shape((8, LANES), F32),
         ),
-    )(table_rows, accum, partial_sum, other, asked)
-    moved = exchange(moved)
-
-    group = 16
-    found = call(
-        functools.partial(found_kernel, group),
-        "found",
-        2**32,
-        2**22,
-        grid=(shards // group,),
-        in_specs=[whole(moved.shape)],
-        out_specs=pl.BlockSpec((group, req_slots, width), lambda g: (g, 0, 0)),
-        out_shape=shape((shards, req_slots, width), BF16),
         scratch_shapes=[
+            pltpu.VMEM(table_rows.shape, F32),
+            pltpu.VMEM(table_rows.shape, F32),
+            pltpu.VMEM(table_rows.shape, BF16),
             pltpu.VMEM((512, 512), BF16),
-            pltpu.VMEM((LANES, LANES), F32),
-            ex,
+            pltpu.SemaphoreType.DMA((2,)),
         ],
-    )(moved)
-    returned = exchange(found)
+    )(table_rows, accum, partial_sum, other, picks)
+    returned = exchange(sent)
 
     place_rows = rows_dev // LANES
     own_places = lax.dynamic_slice_in_dim(
         places, lax.axis_index("shard") * place_rows, place_rows, axis=0
     )
-    serving_rows = call(
-        serving_kernel,
-        "serving",
-        2**30,
-        2**20,
-        out_shape=shape((rows_dev, width), BF16),
-    )(own_places, moved)
-
-    scores = call(
+    scores, serving_rows = call(
         functools.partial(rank_kernel, group),
         "pool_rank",
         2**32,
         2**22,
         grid=(shards // group,),
         in_specs=[
-            pl.BlockSpec((group, req_slots, width), lambda g: (g, 0, 0)),
-            whole((shards, req_slots)),
+            pl.BlockSpec((group, REQ_SLOTS + block, width), lambda g: (g, 0, 0)),
+            whole((shards, LANES)),
             whole(columns.shape),
+            whole(own_places.shape),
             whole(w_hidden.shape),
             whole((1, hidden_width)),
             whole((1, hidden_width)),
         ],
-        out_specs=whole((1, requests)),
-        out_shape=shape((1, requests), F32),
-        scratch_shapes=[pltpu.VMEM((512, 256), F32)],
-    )(returned, mrow, mcol, w_hidden, b_hidden.reshape(1, -1), w_score.reshape(1, -1))
-    return (new_rows, new_accum, serving_rows, scores.reshape(requests))
+        out_specs=(whole((1, requests)), whole((rows_dev, width))),
+        out_shape=(shape((1, requests), F32), shape((rows_dev, width), BF16)),
+        scratch_shapes=[pltpu.VMEM((512, 256), F32), pltpu.VMEM((4, 512, LANES), BF16)],
+    )(returned, mrow, mcol, own_places, w_hidden, b_hidden.reshape(1, -1), w_score.reshape(1, -1))
+    scores = lax.cond(
+        most[0, 0] <= REQ_SLOTS,
+        lambda: scores.reshape(requests),
+        lambda: range_scores(
+            serving_rows, req_ids, w_hidden, b_hidden, w_score, shards, id_columns // per_field
+        ),
+    )
+    return (new_rows, new_accum, serving_rows, scores)
 
 
 def solution(mesh):

time: 190 us -> 163 us (0.86)
  waiting for transfers between devices: 75 us -> 33.4 us
  blocking collectives: 28.7 us -> 67 us
  Pallas kernels: 63.3 us -> 51.8 us
  starting transfers between devices: 16.9 us -> 5.5 us
    all_to_all x2 -> x1, waiting for transfers between devices: 72.2 us -> 30.7 us  [exchange(): lax.all_to_all(rows, 'shard', split_axis=0, concat_axis=0, tiled=True)]
    all_to_all x1, blocking collectives: 28.7 us -> 67 us  [exchange(): lax.all_to_all(rows, 'shard', split_axis=0, concat_axis=0, tiled=True)]
    pallas_call x4 -> x1, Pallas kernels: 21 us -> 6.63 us  [on_device(): call(functools.partial(update_kernel, group), 'update', 2 ** 32, 2 ** 23,...]
    all_to_all x2 -> x1, starting transfers between devices: 16.9 us -> 5.42 us  [exchange(): lax.all_to_all(rows, 'shard', split_axis=0, concat_axis=0, tiled=True)]
    pallas_call x1, Pallas kernels: 11.2 us -> 15.3 us  [on_device(): call(functools.partial(index_kernel, shards, rows_dev, per_field, groups)...]
    pallas_call x1, Pallas kernels: 15.3 us -> 13.2 us  [on_device(): call(functools.partial(sum_kernel, group), 'gradient_sum', 2 ** 33, 2 **...]
  transfers between devices with their start and end apart: 3 -> 2, of which waited for: 3 -> 2; matrix products, arithmetic and copies ran while one was open for 1% -> 1% of each run, Pallas kernels for 5% -> 0%
where the time goes in v2:
time: 163 us; the launch traced here: 162 us
  blocking collectives  67 us (41%)
  Pallas kernels  51.8 us (32%)
  waiting for transfers between devices  33.4 us (20%)
  starting transfers between devices  5.5 us (3%)
  local copies, waits for them, and re-layouts  3.09 us (2%)
    all_to_all x1, blocking collectives, exchange(): lax.all_to_all(rows, 'shard', split_axis=0, concat_axis=0, tiled=True)  67 us
    all_to_all x1, waiting for transfers between devices, exchange(): lax.all_to_all(rows, 'shard', split_axis=0, concat_axis=0, tiled=True)  30.7 us
    pallas_call x1, Pallas kernels, on_device(): call(functools.partial(index_kernel, shards, rows_dev, per_field, groups)...  15.3 us
    pallas_call x1, Pallas kernels, on_device(): call(functools.partial(sum_kernel, group), 'gradient_sum', 2 ** 33, 2 **...  13.2 us
    pallas_call x1, Pallas kernels, on_device(): call(functools.partial(build_kernel, group, shards), 'build', 2 ** 33, 2...  8.56 us
    pallas_call x1, Pallas kernels, on_device(): call(functools.partial(rank_kernel, group), 'pool_rank', 2 ** 32, 2 ** 22...  8.12 us
    pallas_call x1, Pallas kernels, on_device(): call(functools.partial(update_kernel, group), 'update', 2 ** 32, 2 ** 23,...  6.63 us
    all_to_all x1, starting transfers between devices, exchange(): lax.all_to_all(rows, 'shard', split_axis=0, concat_axis=0, tiled=True)  5.42 us
  transfers between devices with their start and end apart: 2, of which 2 were waited for; matrix products, arithmetic and copies ran while one was open for 1% of the time, Pallas kernels for 0%

profile of v2, /device:TPU:0, one launch (start us, length us, event | category | flops | bytes accessed | tf_op | source)
XLA Modules:
  0.0 162.2 jit_solution(17547138774121157103)
XLA Ops:
  0.6 1.3 reshape.196.req_ref
  1.9 15.3 %index.1 = (f32[4,128,32]{2,1,0:T(8,128)}, s32[64,128]{1,0:T(8,128)}, bf16[1024,128]{1,0:T(8,128)(2,1)}, s32[64,128]{1,0:T(8,128)}, f32[128,128]{1,0:T(8,128)}) custom-call(s32[32,256]{1,0:T(8,128)} %bitcast.49, s32[1024,128]{1,0:T(8,128)} %bitcast.47, s32[16,256]{1,0:T(8,128)} %reshape.196.req_ref), custom_call_target="tpu_custom_call" | custom-call | flops 8589934592 | bytes 2097152 | tf_op jit(solution)/shard_map/index/pallas_call | solution.py:471
  17.3 8.6 %build.1 = bf16[64,272,128]{2,1,0:T(8,128)(2,1)} custom-call(s32[64,128]{1,0:T(8,128)} %get-tuple-element.36.off_ref, f32[4,128,32]{2,1,0:T(8,128)} %get-tuple-element.37.col_ref, bf16[256,1024]{1,0:T(8,128)(2,1)} %grads_ref.1, bf16[1024,128]{1,0:T(8,128)(2,1)} %get-tuple-element.38.extra_ref), custom_call_target="tpu_custom_call" | custom-call | flops 8589934592 | bytes 4194304 | tf_op jit(solution)/shard_map/build/pallas_call | solution.py:495
  25.8 67.0 %all_to_all.22.got_ref.extra_ref = bf16[64,272,128]{2,1,0:T(8,128)(2,1)S(1)} all-to-all(bf16[64,272,128]{2,1,0:T(8,128)(2,1)} %build.1), channel_id=1, replica_groups=mesh['rep'=2,'shard'=64] {'shard'}, dimensions={0} | all-to-all | bytes 8912896 | tf_op jit(solution)/shard_map/all_to_all | solution.py:439
  92.8 0.0 copy-start
  92.8 0.0 copy-start.1
  92.8 13.2 %gradient_sum.1 = (f32[2056,128]{1,0:T(8,128)S(1)}, f32[128,128]{1,0:T(8,128)S(1)}) custom-call(bf16[64,272,128]{2,1,0:T(8,128)(2,1)S(1)} %all_to_all.22.got_ref.extra_ref, bf16[64,272,128]{2,1,0:T(8,128)(2,1)S(1)} %all_to_all.22.got_ref.extra_ref), custom_call_target="tpu_custom_call" | custom-call | flops 8589934592 | bytes 4194304 | tf_op jit(solution)/shard_map/gradient_sum/pallas_call | solution.py:515
  106.1 0.1 collective-permute-start
  106.2 2.7 %collective-permute-done.two_ref = f32[2056,128]{1,0:T(8,128)S(1)} collective-permute-done((f32[2056,128]{1,0:T(8,128)S(1)}, f32[2056,128]{1,0:T(8,128)S(1)}, u32[]{:S(2)}, u32[]{:S(2)}) %collective-permute-start) | collective-permute-done | bytes 1052704 | tf_op jit(solution)/shard_map/ppermute | solution.py:534
  108.8 0.0 copy-done
  108.8 0.0 copy-done.1
  108.8 6.6 %update.1 = (f32[2048,128]{1,0:T(8,128)}, f32[2048,128]{1,0:T(8,128)}, bf16[64,144,128]{2,1,0:T(8,128)(2,1)}, f32[8,128]{1,0:T(8,128)S(1)}) custom-call(f32[2048,128]{1,0:T(8,128)S(1)} %copy-done, f32[2048,128]{1,0:T(8,128)S(1)} %copy-done.1, f32[2056,128]{1,0:T(8,128)S(1)} %get-tuple-element.39.one_ref, f32[2056,128]{1,0:T(8,128)S(1)} %collective-permute-done.two_ref, ...), custom_call_target="tpu_custom_call" | custom-call | flops 4294967296 | bytes 8388608 | tf_op jit(solution)/shard_map/update/pallas_call | solution.py:539
  115.5 0.0 copy-start.5
  115.5 0.0 copy-start.2
  115.5 0.0 copy-start.3
  115.5 0.0 copy-start.6
  115.5 5.4 %all-to-all-start.3 = ((bf16[64,144,128]{2,1,0:T(8,128)(2,1)}), bf16[64,144,128]{2,1,0:T(8,128)(2,1)S(1)}, u32[]{:S(2)}, u32[]{:S(2)}) async-start(bf16[64,144,128]{2,1,0:T(8,128)(2,1)} %get-tuple-element.43), calls=%async_computation.3 | async-start | bytes 4718592 | tf_op jit(solution)/shard_map/all_to_all | solution.py:439
  120.9 0.0 copy-done.5
  120.9 0.7 constant_dynamic-slice_fusion.place_ref
  121.7 0.5 slice.9
  122.8 30.7 %all-to-all-done.3.ret_ref = bf16[64,144,128]{2,1,0:T(8,128)(2,1)S(1)} async-done(((bf16[64,144,128]{2,1,0:T(8,128)(2,1)}), bf16[64,144,128]{2,1,0:T(8,128)(2,1)S(1)}, u32[]{:S(2)}, u32[]{:S(2)}) %all-to-all-start.3) | async-done | bytes 2359328 | tf_op jit(solution)/shard_map/all_to_all | solution.py:439
  153.6 0.0 copy-done.2
  153.6 0.0 copy-done.3
  153.6 0.0 copy-done.6
  153.6 0.0 copy-start.4
  153.6 8.1 %pool_rank.1 = (f32[1,128]{1,0:T(1,128)S(1)}, bf16[2048,128]{1,0:T(8,128)(2,1)}) custom-call(bf16[64,144,128]{2,1,0:T(8,128)(2,1)S(1)} %all-to-all-done.3.ret_ref, s32[64,128]{1,0:T(8,128)S(1)} %copy-done.3, f32[128,128]{1,0:T(8,128)S(1)} %copy-done.2, s32[16,128]{1,0:T(8,128)S(1)} %constant_dynamic-slice_fusion.place_ref, bf16[1024,1024]{1,0:T(8,128)(2,1)} %w_ref.1, ...), custom_call_target="tpu_custom_call" | custom-call | flops 4294967296 | bytes 4194304 | tf_op jit(solution)/shard_map/pool_rank/pallas_call | solution.py:578
  161.7 0.0 copy-done.4
  161.7 0.0 copy-start.7
  161.7 0.5 copy-done.7
  (2 shorter events, 0.0 us)
Async XLA Ops:
  92.8 16.0 %copy-start = (f32[2048,128]{1,0:T(8,128)S(1)}, f32[2048,128]{1,0:T(8,128)}, u32[]{:S(2)}) copy-start(f32[2048,128]{1,0:T(8,128)} %table_ref.1) | copy-start | bytes 3145732
  92.8 16.0 %copy-start.1 = (f32[2048,128]{1,0:T(8,128)S(1)}, f32[2048,128]{1,0:T(8,128)}, u32[]{:S(2)}) copy-start(f32[2048,128]{1,0:T(8,128)} %accum_ref.1) | copy-start | bytes 3145732
  106.1 2.7 %collective-permute-start = (f32[2056,128]{1,0:T(8,128)S(1)}, f32[2056,128]{1,0:T(8,128)S(1)}, u32[]{:S(2)}, u32[]{:S(2)}) collective-permute-start(f32[2056,128]{1,0:T(8,128)S(1)} %get-tuple-element.39.one_ref), channel_id=1, source_target_pairs={{0,64},{64,0},{1,65},{65,1},{2,66},{66,2},{3,67},{67,3},{4,68},{68... | collective-permute-start | bytes 3158024 | tf_op jit(solution)/shard_map/ppermute | solution.py:534
  115.5 5.5 %copy-start.5 = (bf16[1024]{0:T(1024)(128)(2,1)S(1)}, bf16[1024]{0:T(1024)(128)(2,1)}, u32[]{:S(2)}) copy-start(bf16[1024]{0:T(1024)(128)(2,1)} %param.20) | copy-start | bytes 6148
  115.5 38.1 %copy-start.2 = (f32[128,128]{1,0:T(8,128)S(1)}, f32[128,128]{1,0:T(8,128)}, u32[]{:S(2)}) copy-start(f32[128,128]{1,0:T(8,128)} %get-tuple-element.45.mcol_ref) | copy-start | bytes 196612
  115.5 38.1 %copy-start.3 = (s32[64,128]{1,0:T(8,128)S(1)}, s32[64,128]{1,0:T(8,128)}, u32[]{:S(2)}) copy-start(s32[64,128]{1,0:T(8,128)} %get-tuple-element.44.mrow_ref) | copy-start | bytes 98308
  115.5 38.1 %copy-start.6 = (f32[1024]{0:T(1024)S(1)}, f32[1024]{0:T(1024)}, u32[]{:S(2)}) copy-start(f32[1024]{0:T(1024)} %param.19) | copy-start | bytes 12292
  115.5 38.1 %all-to-all-start.3 = ((bf16[64,144,128]{2,1,0:T(8,128)(2,1)}), bf16[64,144,128]{2,1,0:T(8,128)(2,1)S(1)}, u32[]{:S(2)}, u32[]{:S(2)}) async-start(bf16[64,144,128]{2,1,0:T(8,128)(2,1)} %get-tuple-element.43), calls=%async_computation.3 | async-start | bytes 4718592 | tf_op jit(solution)/shard_map/all_to_all | solution.py:439
  153.6 8.1 %copy-start.4 = (s32[128,32]{0,1:T(8,128)S(1)}, s32[128,32]{0,1:T(8,128)}, u32[]{:S(2)}) copy-start(s32[128,32]{0,1:T(8,128)} %param.17) | copy-start | bytes 49156
  161.7 0.5 copy-start.7

commit v3 on v2

--- a/solution.py
+++ b/solution.py
@@ -9,7 +9,7 @@
 
 F32, BF16, I32 = jnp.float32, jnp.bfloat16, jnp.int32
 NT = (((1,), (1,)), ((), ()))
-SMALL, LARGE = 32 * 2**20, 60 * 2**20
+VMEM_LIMIT = 32 * 2**20
 EXTRA = 16
 LANES = 128
 REQ_SLOTS = 112
@@ -72,57 +72,141 @@
     hot = ones_where(iota((lines, count), 0) == (line & (lines - 1)))
     low = (ids & 127) + jnp.where(line >= lines, LANES, 0)
     found = jnp.where(iota((lows, count), 0) == low, dot(table, hot), 0.0)
-    value = jnp.sum(found, axis=0, keepdims=True)
-    last = jnp.zeros_like(value)
+    return jnp.sum(found, axis=0, keepdims=True)
+
+
+def unpack(value):
+    last, scale = jnp.zeros_like(value), jnp.ones_like(value)
     for bits in (16, 8, 4, 2, 1):
         big = value >= 64.0 * 2.0**bits
         value = jnp.where(big, value * 2.0**-bits, value)
         last = last + jnp.where(big, float(bits), 0.0)
-    return value - 64.0, last
-
-
-def index_kernel(
+        scale = jnp.where(big, scale * 2.0**bits, scale)
+    return value - 64.0, last, scale
+
+
+def send_kernel(
+    shards, rows_dev, per_field, groups, group,
+    ids_ref, place_ref, req_ref, grads_ref, out_ref, mrow_ref, mcol_ref,
+    ids, places, requests, grads, col, off_vmem, off, extra, rows_scr, sems, *scratch,
+):
+    step = pl.program_id(0)
+
+    @pl.when(step == 0)
+    def _():
+        loads = [
+            pltpu.make_async_copy(source, target, sems.at[at])
+            for at, (source, target) in enumerate(
+                ((place_ref, places), (ids_ref, ids), (req_ref, requests), (grads_ref, grads))
+            )
+        ]
+        for load in loads:
+            load.start()
+        for load in loads[:3]:
+            load.wait()
+        index_ids(
+            shards, rows_dev, per_field, groups,
+            ids, places, requests, col, off_vmem, extra, mrow_ref, mcol_ref, *scratch,
+        )
+        copy = pltpu.make_async_copy(off_vmem, off, sems.at[4])
+        copy.start()
+        loads[3].wait()
+        sort_rows(col, grads, rows_scr)
+        copy.wait()
+
+    fill_slots(step, group, groups, off, extra, rows_scr, out_ref)
+
+
+def index_ids(
     shards, rows_dev, per_field, groups,
     ids_ref, place_ref, req_ref, col_ref, off_ref, extra_ref, mrow_ref, mcol_ref,
-    table, ex, own_scr, rank_scr, mark, off_scr,
+    table, ex, values, owners, scales, rank_scr, mark, off_scr,
 ):
     shift = rows_dev.bit_length() - 1
     width = ids_ref.shape[1]
     count = per_field * width
     fields = ids_ref.shape[0] // per_field
     span = fields // groups
+    batch = count // req_ref.shape[1]
+    batches = req_ref.shape[0] // batch
     table[...] = pack_places(place_ref[...], shift, rows_dev // shards)
     tri = strict_upper(width)
     ones = jnp.ones((width, LANES), BF16)
 
+    def train_look_up(c, unused):
+        ids = lanes_of(ids_ref, c * per_field, per_field)
+        values[pl.ds(c, 1), :] = look_up(table[...], ids)
+        return unused
+
+    def request_look_up(c, unused):
+        ids = lanes_of(req_ref, c * batch, batch)
+        values[pl.ds(fields + c, 1), :] = look_up(table[...], ids)
+        return unused
+
+    values[...] = jnp.zeros_like(values)
+    lax.fori_loop(0, fields, train_look_up, 0, unroll=4)
+    lax.fori_loop(0, batches, request_look_up, 0, unroll=4)
+    owner, unused, scale = unpack(values[...])
+    owners[...] = owner
+    scales[...] = scale
+
+    def packed(ids, at):
+        return ((ids >> shift) + 64).astype(F32) * scales[pl.ds(at, 1), :]
+
     def field_step(field, carry):
         base, row = carry
         ids = lanes_of(ids_ref, field * per_field, per_field)
-        owner, last = look_up(table[...], ids)
         mark[pl.ds(field * shards, shards), :] = base
-        own, rank, base = rank_ids(owner, base, shards, tri, ones)
-        own_scr[pl.ds(field, 1), :] = owner
+        own, rank, base = rank_ids(owners[pl.ds(field, 1), :], base, shards, tri, ones)
         rank_scr[pl.ds(field, 1), :] = rank
         at = ones_where(iota((width, count), 0, F32) == rank)
-        target = jnp.concatenate([own * (ids >> shift).astype(F32), own * last], axis=0)
-        row = row + dot_nt(target.astype(BF16), at)
-        return base, row
+        return base, row + dot_nt((own * packed(ids, field)).astype(BF16), at)
 
     base, row = lax.fori_loop(
         0,
         fields,
         field_step,
-        (jnp.zeros((shards, LANES), F32), jnp.zeros((2 * shards, width), F32)),
+        (jnp.zeros((shards, LANES), F32), jnp.zeros((shards, width), F32)),
+        unroll=4,
     )
     mark[fields * shards :, :] = base
+
+    lane = iota((1, count), 1)
+
+    def request_step(c, carry):
+        base, row = carry
+        ids = lanes_of(req_ref, c * batch, batch)
+        own, rank, base = rank_ids(owners[pl.ds(fields + c, 1), :], base, shards, tri, ones)
+        at = ones_where(iota((LANES, count), 0, F32) == jnp.where(rank < REQ_SLOTS, rank, -1.0))
+        field = c * (batch // per_field) + lane // (per_field * LANES)
+        digits = [
+            own * packed(ids, fields + c),
+            own * (lane & (LANES - 1)).astype(F32),
+            own * (field + 1).astype(F32),
+        ]
+        return base, row + dot_nt(jnp.concatenate(digits, axis=0).astype(BF16), at)
+
+    most, asked = lax.fori_loop(
+        0,
+        batches,
+        request_step,
+        (jnp.zeros((shards, LANES), F32), jnp.zeros((3 * shards, LANES), F32)),
+        unroll=4,
+    )
+    most = jnp.minimum(jnp.max(most, axis=0, keepdims=True), 255.0)
+    parts = [
+        row[:, :LANES], row[:, LANES:], asked[:shards], jnp.broadcast_to(most, (shards, LANES))
+    ]
     ex[...] = jnp.zeros_like(ex)
-    for kind in range(2):
-        for half in range(2):
-            ex[pl.ds(2 * kind + half, shards, stride=EXTRA), :] = row[
-                kind * shards : (kind + 1) * shards, half * LANES : (half + 1) * LANES
-            ]
-    index_requests(shards, shift, req_ref, table, ex, mrow_ref, mcol_ref)
+    for kind, part in enumerate(parts):
+        ex[pl.ds(kind, shards, stride=EXTRA), :] = part
     extra_ref[...] = ex[...].astype(BF16)
+    number = asked[2 * shards :]
+    field = number.astype(I32) - 1
+    mrow_ref[...] = jnp.where(
+        field < 0, -1, (field & 3) * LANES + asked[shards : 2 * shards].astype(I32)
+    )
+    mcol_ref[...] = jnp.where(jnp.concatenate([number, number], axis=0).T > 4.0, 1.0, 0.0)
 
     earlier = ones_where(iota((shards, shards), 1) < iota((shards, shards), 0))
     lane = iota((shards, LANES), 1)
@@ -143,7 +227,7 @@
     field = (at // count).astype(F32)
 
     def group_step(g, unused):
-        owner = lanes_of(own_scr, g * span, span)
+        owner = lanes_of(owners, g * span, span)
         off = off_scr[pl.ds(g * shards, shards), :]
         shifts = jnp.where(
             iota((shards, total), 0, F32) == owner,
@@ -159,87 +243,57 @@
         col_ref[g] = dot_nt(ones_where(iota((LANES, total), 0) == (pos & 127)), source)
         return unused
 
-    lax.fori_loop(0, groups, group_step, 0)
-
-
-def index_requests(shards, shift, req_ref, table, ex, mrow_ref, mcol_ref):
-    width = req_ref.shape[1]
-    batch = 4
-    count = batch * width
-    tri = strict_upper(width)
-    ones = jnp.ones((width, LANES), BF16)
-    lane = iota((1, count), 1)
-
-    def step(c, carry):
-        base, row, col = carry
-        ids = lanes_of(req_ref, c * batch, batch)
-        owner, last = look_up(table[...], ids)
-        own, rank, base = rank_ids(owner, base, shards, tri, ones)
-        at = ones_where(iota((LANES, count), 0, F32) == jnp.where(rank < REQ_SLOTS, rank, -1.0))
-        field = c * (batch // 2) + lane // (2 * width)
-        query = (own * (lane & (LANES - 1)).astype(F32)).astype(BF16)
-        number = (own * (field + 1).astype(F32)).astype(BF16)
-        high = (own * (ids >> shift).astype(F32)).astype(BF16)
-        low = (own * last).astype(BF16)
-        row = row + dot_nt(jnp.concatenate([high, low, query, number], axis=0), at)
-        col = col + dot_nt(at, jnp.concatenate([number, number], axis=0))
-        return base, row, col
-
-    base, row, col = lax.fori_loop(
-        0,
-        req_ref.shape[0] // batch,
-        step,
-        (
-            jnp.zeros((shards, LANES), F32),
-            jnp.zeros((4 * shards, LANES), F32),
-            jnp.zeros((LANES, 2 * shards), F32),
-        ),
-    )
-    most = jnp.broadcast_to(jnp.max(base, axis=0, keepdims=True), (shards, LANES)).astype(I32)
-    parts = [row[:shards], row[shards : 2 * shards], (most >> 5).astype(F32), (most & 31).astype(F32)]
-    for kind, part in enumerate(parts):
-        ex[pl.ds(4 + kind, shards, stride=EXTRA), :] = part
-    field = row[3 * shards :].astype(I32) - 1
-    mrow_ref[...] = jnp.where(
-        field < 0, -1, (field & 3) * LANES + row[2 * shards : 3 * shards].astype(I32)
-    )
-    mcol_ref[...] = jnp.where(col > 4.0, 1.0, 0.0)
-
-
-def build_kernel(group, shards, off_ref, col_ref, grads_ref, extra_ref, out_ref, rows_scr):
-    slots = out_ref.shape[1] - EXTRA
+    lax.fori_loop(0, groups, group_step, 0, unroll=4)
+
+
+def index_scratch(samples, id_columns, per_field, groups, shards, lines):
+    fields = id_columns // per_field
+    count = per_field * samples
+    return [
+        pltpu.VMEM((2 * LANES, lines // 2), BF16),
+        pltpu.VMEM((shards * EXTRA, LANES), F32),
+        pltpu.VMEM((2 * fields, count), F32),
+        pltpu.VMEM((2 * fields, count), F32),
+        pltpu.VMEM((2 * fields, count), F32),
+        pltpu.VMEM((fields, count), F32),
+        pltpu.VMEM(((fields + 1) * shards, LANES), F32),
+        pltpu.VMEM((groups * shards, LANES), F32),
+    ]
+
+
+def sort_rows(col_ref, grads_ref, rows_scr):
     samples = grads_ref.shape[0]
     groups = col_ref.shape[0]
     blocks = col_ref.shape[2] // 2
     total = blocks * LANES
+    pad = (rows_scr.shape[1] - total) // 2
     span = grads_ref.shape[1] // groups
-    step = pl.program_id(0)
-
-    @pl.when(step == 0)
-    def _():
-        def sort_group(g, unused):
-            col = col_ref[g]
-            hots = [
-                ones_where(iota((LANES, samples), 1, F32) == col[:, b : b + 1])
+
+    def sort_group(g, unused):
+        col = col_ref[g]
+        hots = [
+            ones_where(iota((LANES, samples), 1, F32) == col[:, b : b + 1]) for b in range(blocks)
+        ]
+        part = grads_ref[:, pl.ds(pl.multiple_of(g * span, span), span)]
+        rows = dot(jnp.concatenate(hots, axis=0), part)
+        field = jnp.concatenate(
+            [
+                jnp.broadcast_to(col[:, blocks + b : blocks + b + 1], (LANES, LANES))
                 for b in range(blocks)
-            ]
-            part = grads_ref[:, pl.ds(pl.multiple_of(g * span, span), span)]
-            rows = dot(jnp.concatenate(hots, axis=0), part)
-            field = jnp.concatenate(
-                [
-                    jnp.broadcast_to(col[:, blocks + b : blocks + b + 1], (LANES, LANES))
-                    for b in range(blocks)
-                ],
-                axis=0,
-            )
-            picked = rows[:, :LANES]
-            for q in range(1, span // LANES):
-                picked = jnp.where(field == float(q), rows[:, q * LANES : (q + 1) * LANES], picked)
-            rows_scr[g, slots : slots + total, :] = picked
-            return unused
-
-        lax.fori_loop(0, groups, sort_group, 0)
-
+            ],
+            axis=0,
+        )
+        picked = rows[:, :LANES]
+        for q in range(1, span // LANES):
+            picked = jnp.where(field == float(q), rows[:, q * LANES : (q + 1) * LANES], picked)
+        rows_scr[g, pad : pad + total, :] = picked
+        return unused
+
+    lax.fori_loop(0, groups, sort_group, 0)
+
+
+def fill_slots(step, group, groups, off_ref, extra_ref, rows_scr, out_ref):
+    slots = out_ref.shape[1] - EXTRA
     at = iota((slots, LANES), 0)
 
     def one(b, unused):
@@ -251,7 +305,9 @@
             picked = jnp.where(at >= start, rows, picked)
         picked = jnp.where(at >= off_ref[owner, 2 * groups - 1], 0.0, picked)
         out_ref[b, 0:slots, :] = picked.astype(BF16)
-        out_ref[b, slots : slots + EXTRA, :] = extra_ref[pl.ds(b * EXTRA, EXTRA), :]
+        out_ref[b, slots : slots + EXTRA, :] = extra_ref[
+            pl.ds(pl.multiple_of(owner * EXTRA, EXTRA), EXTRA), :
+        ]
         return unused
 
     lax.fori_loop(0, group, one, 0, unroll=4)
@@ -265,18 +321,19 @@
     @pl.when(step == 0)
     def _():
         scr[...] = extra_ref[...].astype(F32).reshape(scr.shape)
-        lows = []
+        kinds = [scr[pl.ds(kind, shards, stride=EXTRA), :] for kind in range(4)]
+        first, last, unused = unpack(jnp.concatenate(kinds[:3], axis=0))
+        first = jnp.maximum(first, 0.0).astype(I32)
+        high = (first & 15) * 32 + last.astype(I32)
+        low = (first >> 4).astype(F32)
         for half in range(2):
-            ranges = scr[pl.ds(half, shards, stride=EXTRA), :].astype(I32)
-            within = scr[pl.ds(2 + half, shards, stride=EXTRA), :].astype(I32)
-            hi_scr[half] = (ranges & 15) * 32 + within
-            lows.append((ranges >> 4).astype(F32))
-        lo_scr[...] = jnp.concatenate(lows, axis=0).T
+            hi_scr[half] = high[half * shards : (half + 1) * shards]
+        lo_scr[...] = low[: 2 * shards].T
         total[...] = jnp.zeros_like(total)
-        kinds = [scr[pl.ds(kind, shards, stride=EXTRA), :].astype(I32) for kind in range(4, 8)]
-        high = (kinds[0] & 15) * 32 + kinds[1]
-        picks_ref[...] = jnp.concatenate([high, kinds[0] >> 4], axis=0).astype(F32).T
-        most = jnp.max((kinds[2] * 32 + kinds[3]).astype(F32), axis=0, keepdims=True)
+        picks_ref[...] = jnp.concatenate(
+            [high[2 * shards :].astype(F32), low[2 * shards :]], axis=0
+        ).T
+        most = jnp.max(kinds[3], axis=0, keepdims=True)
         out_ref[4 * 512 :, :] = jnp.broadcast_to(most, (8, LANES))
 
     turned = pltpu.roll(lo_scr[...], lax.rem(2 * shards - step * group, 2 * shards), 1)
@@ -354,12 +411,14 @@
 
 def rank_kernel(
     group, ret_ref, mrow_ref, mcol_ref, place_ref, w_ref, b_ref, score_ref, out_ref, serving_ref,
-    total, wide,
+    total, wide, weights, sem,
 ):
     step = pl.program_id(0)
+    load = pltpu.make_async_copy(w_ref, weights, sem)
 
     @pl.when(step == 0)
     def _():
+        load.start()
         total[...] = jnp.zeros_like(total)
 
     turned = pltpu.roll(mcol_ref[...], lax.rem(LANES - step * group, LANES), 1)
@@ -385,7 +444,8 @@
             ],
             axis=1,
         ).astype(BF16)
-        hidden = jnp.maximum(dot(pooled, w_ref[...]) + b_ref[...], 0.0).astype(BF16)
+        load.wait()
+        hidden = jnp.maximum(dot(pooled, weights[...]) + b_ref[...], 0.0).astype(BF16)
         out_ref[...] = dot_nt(score_ref[...], hidden)
         place = place_ref[...]
         owner, last = place >> 11, place & 31
@@ -425,14 +485,18 @@
     return pl.BlockSpec(shape, lambda *step: (0,) * len(shape))
 
 
-def call(kernel, name, flops, moved, limit=SMALL, **kwargs):
+def call(kernel, name, flops, moved, **kwargs):
     return pl.pallas_call(
         kernel,
         name=name,
-        compiler_params=pltpu.CompilerParams(vmem_limit_bytes=limit),
+        compiler_params=pltpu.CompilerParams(vmem_limit_bytes=VMEM_LIMIT),
         cost_estimate=pl.CostEstimate(flops=flops, bytes_accessed=moved, transcendentals=0),
         **kwargs,
     )
+
+
+def in_hbm(array):
+    return pltpu.with_memory_space_constraint(array, pltpu.HBM)
 
 
 def exchange(rows):
@@ -459,59 +523,49 @@
     hidden_width = w_hidden.shape[1]
     per_field = id_columns * width // sample_grads.shape[1]
     block = rows_dev // shards
-    groups = 4
+    groups = 2
     sorted_rows = samples * id_columns // groups
     places = hash_place.reshape(-1, LANES)
     shape = jax.ShapeDtypeStruct
     extras = shape((shards * EXTRA, LANES), BF16)
     columns = shape((LANES, 2 * shards), F32)
-    table = pltpu.VMEM((2 * LANES, places.shape[0] // 2), BF16)
     ex = pltpu.VMEM(extras.shape, F32)
 
-    col, off, extra, mrow, mcol = call(
-        functools.partial(index_kernel, shards, rows_dev, per_field, groups),
-        "index",
-        2**33,
-        2**21,
-        LARGE,
+    group = 16
+    sent, mrow, mcol = call(
+        functools.partial(send_kernel, shards, rows_dev, per_field, groups, group),
+        "send",
+        2**34,
+        2**23,
+        grid=(shards // group,),
+        in_specs=[pl.BlockSpec(memory_space=pl.ANY)] * 4,
+        out_specs=(
+            pl.BlockSpec((group, slots + EXTRA, width), lambda g: (g, 0, 0)),
+            whole((shards, LANES)),
+            whole(columns.shape),
+        ),
         out_shape=(
-            shape((groups, LANES, 2 * sorted_rows // LANES), F32),
-            shape((shards, LANES), I32),
-            extras,
+            shape((shards, slots + EXTRA, width), BF16),
             shape((shards, LANES), I32),
             columns,
         ),
         scratch_shapes=[
-            table,
-            ex,
-            pltpu.VMEM((id_columns // per_field, per_field * samples), F32),
-            pltpu.VMEM((id_columns // per_field, per_field * samples), F32),
-            pltpu.VMEM(((id_columns // per_field + 1) * shards, LANES), F32),
-            pltpu.VMEM((groups * shards, LANES), F32),
-        ],
-    )(sample_ids.T, places, req_ids.T.reshape(-1, 2 * requests))
+            pltpu.VMEM((id_columns, samples), I32),
+            pltpu.VMEM(places.shape, I32),
+            pltpu.VMEM((id_columns, requests), I32),
+            pltpu.VMEM(sample_grads.shape, BF16),
+            pltpu.VMEM((groups, LANES, 2 * sorted_rows // LANES), F32),
+            pltpu.VMEM((shards, LANES), I32),
+            pltpu.SMEM((shards, LANES), I32),
+            pltpu.VMEM(extras.shape, BF16),
+            pltpu.VMEM((groups, sorted_rows + 2 * slots, width), F32),
+            pltpu.SemaphoreType.DMA((5,)),
+        ]
+        + index_scratch(samples, id_columns, per_field, groups, shards, places.shape[0]),
+    )(*[in_hbm(array) for array in (sample_ids.T, places, req_ids.T, sample_grads)])
+    got = exchange(sent)
 
     group = 16
-    sent = call(
-        functools.partial(build_kernel, group, shards),
-        "build",
-        2**33,
-        2**22,
-        LARGE,
-        grid=(shards // group,),
-        in_specs=[
-            pl.BlockSpec(memory_space=pltpu.SMEM),
-            whole(col.shape),
-            whole(sample_grads.shape),
-            pl.BlockSpec((group * EXTRA, LANES), lambda g: (g, 0)),
-        ],
-        out_specs=pl.BlockSpec((group, slots + EXTRA, width), lambda g: (g, 0, 0)),
-        out_shape=shape((shards, slots + EXTRA, width), BF16),
-        scratch_shapes=[pltpu.VMEM((groups, sorted_rows + 2 * slots, width), F32)],
-    )(off, col, sample_grads, extra)
-    got = exchange(sent)
-
-    group = 8
     partial_sum, picks = call(
         functools.partial(sum_kernel, group),
         "gradient_sum",
@@ -533,7 +587,7 @@
     )(got, got)
     other = lax.ppermute(partial_sum, "rep", [(0, 1), (1, 0)])
 
-    group = 16
+    group = 32
     rows_type = shape((rows_dev, width), F32)
     any_space = pl.BlockSpec(memory_space=pl.ANY)
     new_rows, new_accum, sent, most = call(
@@ -575,6 +629,7 @@
     own_places = lax.dynamic_slice_in_dim(
         places, lax.axis_index("shard") * place_rows, place_rows, axis=0
     )
+    group = 16
     scores, serving_rows = call(
         functools.partial(rank_kernel, group),
         "pool_rank",
@@ -586,14 +641,22 @@
             whole((shards, LANES)),
             whole(columns.shape),
             whole(own_places.shape),
-            whole(w_hidden.shape),
+            pl.BlockSpec(memory_space=pl.ANY),
             whole((1, hidden_width)),
             whole((1, hidden_width)),
         ],
         out_specs=(whole((1, requests)), whole((rows_dev, width))),
-        out_shape=(shape((1, requests), F32), shape((rows_dev, width), BF16)),
-        scratch_shapes=[pltpu.VMEM((512, 256), F32), pltpu.VMEM((4, 512, LANES), BF16)],
-    )(returned, mrow, mcol, own_places, w_hidden, b_hidden.reshape(1, -1), w_score.reshape(1, -1))
+        out_shape=(pltpu.HBM((1, requests), F32), shape((rows_dev, width), BF16)),
+        scratch_shapes=[
+            pltpu.VMEM((512, 256), F32),
+            pltpu.VMEM((4, 512, LANES), BF16),
+            pltpu.VMEM(w_hidden.shape, BF16),
+            pltpu.SemaphoreType.DMA,
+        ],
+    )(
+        returned, mrow, mcol, own_places, in_hbm(w_hidden),
+        b_hidden.reshape(1, -1), w_score.reshape(1, -1),
+    )
     scores = lax.cond(
         most[0, 0] <= REQ_SLOTS,
         lambda: scores.reshape(requests),

time: 163 us -> 151 us (0.926)
  Pallas kernels: 51.8 us -> 41.6 us
    pallas_call x2 -> x1, Pallas kernels: 23.9 us -> 17 us  [on_device(): call(functools.partial(send_kernel, shards, rows_dev, per_field, groups,...]
where the time goes in v3:
time: 151 us
  blocking collectives  66.8 us (44%)
  Pallas kernels  41.6 us (28%)
  waiting for transfers between devices  33.4 us (22%)
  starting transfers between devices  5.29 us (4%)
  local copies, waits for them, and re-layouts  2.4 us (2%)
    all_to_all x1, blocking collectives, exchange(): lax.all_to_all(rows, 'shard', split_axis=0, concat_axis=0, tiled=True)  66.8 us
    all_to_all x1, waiting for transfers between devices, exchange(): lax.all_to_all(rows, 'shard', split_axis=0, concat_axis=0, tiled=True)  30.7 us
    pallas_call x1, Pallas kernels, on_device(): call(functools.partial(send_kernel, shards, rows_dev, per_field, groups,...  17 us
    pallas_call x1, Pallas kernels, on_device(): call(functools.partial(sum_kernel, group), 'gradient_sum', 2 ** 33, 2 **...  11.9 us
    pallas_call x1, Pallas kernels, on_device(): call(functools.partial(rank_kernel, group), 'pool_rank', 2 ** 32, 2 ** 22...  6.56 us
    pallas_call x1, Pallas kernels, on_device(): call(functools.partial(update_kernel, group), 'update', 2 ** 32, 2 ** 23,...  6.19 us
    all_to_all x1, starting transfers between devices, exchange(): lax.all_to_all(rows, 'shard', split_axis=0, concat_axis=0, tiled=True)  5.21 us
  transfers between devices with their start and end apart: 2, of which 2 were waited for; matrix products, arithmetic and copies ran while one was open for 1% of the time, Pallas kernels for 0%

profile of v3, /device:TPU:0, one launch (start us, length us, event | category | flops | bytes accessed | tf_op | source)
XLA Modules:
  0.0 150.9 jit_solution(10528324049568084549)
XLA Ops:
  0.6 17.0 %send.1 = (bf16[64,272,128]{2,1,0:T(8,128)(2,1)S(1)}, s32[64,128]{1,0:T(8,128)S(1)}, f32[128,128]{1,0:T(8,128)S(1)}) custom-call(s32[32,256]{1,0:T(8,128)} %bitcast.49, s32[1024,128]{1,0:T(8,128)} %bitcast.47, s32[32,128]{1,0:T(8,128)} %bitcast.45, bf16[256,1024]{1,0:T(8,128)(2,1)} %grads_ref.1), custom_call_target="tpu_custom_call" | custom-call | flops 17179869184 | bytes 8388608 | tf_op jit(solution)/shard_map/send/pallas_call | solution.py:535
  17.6 66.8 %all_to_all.22.got_ref.extra_ref = bf16[64,272,128]{2,1,0:T(8,128)(2,1)S(1)} all-to-all(bf16[64,272,128]{2,1,0:T(8,128)(2,1)S(1)} %get-tuple-element.34), channel_id=1, replica_groups=mesh['rep'=2,'shard'=64] {'shard'}, dimensions={0} | all-to-all | bytes 8912896 | tf_op jit(solution)/shard_map/all_to_all | solution.py:503
  84.4 0.0 copy-start
  84.4 0.0 copy-start.1
  84.4 11.9 %gradient_sum.1 = (f32[2056,128]{1,0:T(8,128)S(1)}, f32[128,128]{1,0:T(8,128)S(1)}) custom-call(bf16[64,272,128]{2,1,0:T(8,128)(2,1)S(1)} %all_to_all.22.got_ref.extra_ref, bf16[64,272,128]{2,1,0:T(8,128)(2,1)S(1)} %all_to_all.22.got_ref.extra_ref), custom_call_target="tpu_custom_call" | custom-call | flops 8589934592 | bytes 4194304 | tf_op jit(solution)/shard_map/gradient_sum/pallas_call | solution.py:569
  96.3 0.1 collective-permute-start
  96.4 2.7 %collective-permute-done.two_ref = f32[2056,128]{1,0:T(8,128)S(1)} collective-permute-done((f32[2056,128]{1,0:T(8,128)S(1)}, f32[2056,128]{1,0:T(8,128)S(1)}, u32[]{:S(2)}, u32[]{:S(2)}) %collective-permute-start) | collective-permute-done | bytes 1052704 | tf_op jit(solution)/shard_map/ppermute | solution.py:588
  99.0 0.0 copy-done
  99.0 0.0 copy-done.1
  99.0 6.2 %update.1 = (f32[2048,128]{1,0:T(8,128)}, f32[2048,128]{1,0:T(8,128)}, bf16[64,144,128]{2,1,0:T(8,128)(2,1)}, f32[8,128]{1,0:T(8,128)S(1)}) custom-call(f32[2048,128]{1,0:T(8,128)S(1)} %copy-done, f32[2048,128]{1,0:T(8,128)S(1)} %copy-done.1, f32[2056,128]{1,0:T(8,128)S(1)} %get-tuple-element.35.one_ref, f32[2056,128]{1,0:T(8,128)S(1)} %collective-permute-done.two_ref, ...), custom_call_target="tpu_custom_call" | custom-call | flops 4294967296 | bytes 8388608 | tf_op jit(solution)/shard_map/update/pallas_call | solution.py:593
  105.2 0.0 copy-start.3
  105.3 0.0 copy-start.4
  105.3 5.2 %all-to-all-start.3 = ((bf16[64,144,128]{2,1,0:T(8,128)(2,1)}), bf16[64,144,128]{2,1,0:T(8,128)(2,1)S(1)}, u32[]{:S(2)}, u32[]{:S(2)}) async-start(bf16[64,144,128]{2,1,0:T(8,128)(2,1)} %get-tuple-element.39), calls=%async_computation.3 | async-start | bytes 4718592 | tf_op jit(solution)/shard_map/all_to_all | solution.py:503
  110.5 0.0 copy-done.3
  110.5 0.7 constant_dynamic-slice_fusion.place_ref
  111.2 0.5 slice.9
  112.4 30.7 %all-to-all-done.3.ret_ref = bf16[64,144,128]{2,1,0:T(8,128)(2,1)S(1)} async-done(((bf16[64,144,128]{2,1,0:T(8,128)(2,1)}), bf16[64,144,128]{2,1,0:T(8,128)(2,1)S(1)}, u32[]{:S(2)}, u32[]{:S(2)}) %all-to-all-start.3) | async-done | bytes 2359328 | tf_op jit(solution)/shard_map/all_to_all | solution.py:503
  143.1 0.0 copy-done.4
  143.1 0.0 copy-start.2
  143.1 6.6 %pool_rank.1 = (f32[1,128]{1,0:T(1,128)}, bf16[2048,128]{1,0:T(8,128)(2,1)}) custom-call(bf16[64,144,128]{2,1,0:T(8,128)(2,1)S(1)} %all-to-all-done.3.ret_ref, s32[64,128]{1,0:T(8,128)S(1)} %get-tuple-element.40.mrow_ref, f32[128,128]{1,0:T(8,128)S(1)} %get-tuple-element.41.mcol_ref, s32[16,128]{1,0:T(8,128)S(1)} %constant_dynamic-slice_fusion.place_ref, ...), custom_call_target="tpu_custom_call" | custom-call | flops 4294967296 | bytes 4194304 | tf_op jit(solution)/shard_map/pool_rank/pallas_call | solution.py:633
  149.7 0.0 copy-start.5
  149.7 0.0 copy-done.2
  149.7 0.6 copy-done.5
  150.3 0.0 copy-start.6
  150.3 0.5 copy-done.6
  (2 shorter events, 0.0 us)
Async XLA Ops:
  84.4 14.7 %copy-start = (f32[2048,128]{1,0:T(8,128)S(1)}, f32[2048,128]{1,0:T(8,128)}, u32[]{:S(2)}) copy-start(f32[2048,128]{1,0:T(8,128)} %table_ref.1) | copy-start | bytes 3145732
  84.4 14.7 %copy-start.1 = (f32[2048,128]{1,0:T(8,128)S(1)}, f32[2048,128]{1,0:T(8,128)}, u32[]{:S(2)}) copy-start(f32[2048,128]{1,0:T(8,128)} %accum_ref.1) | copy-start | bytes 3145732
  96.3 2.7 %collective-permute-start = (f32[2056,128]{1,0:T(8,128)S(1)}, f32[2056,128]{1,0:T(8,128)S(1)}, u32[]{:S(2)}, u32[]{:S(2)}) collective-permute-start(f32[2056,128]{1,0:T(8,128)S(1)} %get-tuple-element.35.one_ref), channel_id=1, source_target_pairs={{0,64},{64,0},{1,65},{65,1},{2,66},{66,2},{3,67},{67,3},{4,68},{68... | collective-permute-start | bytes 3158024 | tf_op jit(solution)/shard_map/ppermute | solution.py:588
  105.2 5.2 %copy-start.3 = (bf16[1024]{0:T(1024)(128)(2,1)S(1)}, bf16[1024]{0:T(1024)(128)(2,1)}, u32[]{:S(2)}) copy-start(bf16[1024]{0:T(1024)(128)(2,1)} %param.20) | copy-start | bytes 6148
  105.3 37.9 %copy-start.4 = (f32[1024]{0:T(1024)S(1)}, f32[1024]{0:T(1024)}, u32[]{:S(2)}) copy-start(f32[1024]{0:T(1024)} %param.19) | copy-start | bytes 12292
  105.3 37.8 %all-to-all-start.3 = ((bf16[64,144,128]{2,1,0:T(8,128)(2,1)}), bf16[64,144,128]{2,1,0:T(8,128)(2,1)S(1)}, u32[]{:S(2)}, u32[]{:S(2)}) async-start(bf16[64,144,128]{2,1,0:T(8,128)(2,1)} %get-tuple-element.39), calls=%async_computation.3 | async-start | bytes 4718592 | tf_op jit(solution)/shard_map/all_to_all | solution.py:503
  143.1 6.6 %copy-start.2 = (s32[128,32]{0,1:T(8,128)S(1)}, s32[128,32]{0,1:T(8,128)}, u32[]{:S(2)}) copy-start(s32[128,32]{0,1:T(8,128)} %param.17) | copy-start | bytes 49156
  149.7 0.7 copy-start.5
  150.3 0.5 copy-start.6

commit v4 on v3

--- a/solution.py
+++ b/solution.py
@@ -29,6 +29,21 @@
 
 def ones_where(mask):
     return jnp.where(mask, 1.0, 0.0).astype(BF16)
+
+
+def hot_rows(rows, index):
+    short = jnp.broadcast_to(index, (16, index.shape[1])).astype(jnp.int16)
+    at = lax.broadcasted_iota(jnp.int16, (rows, index.shape[1]), 0)
+    match = at == jnp.concatenate([short] * (rows // 16), axis=0)
+    return jnp.where(match, jnp.ones((), BF16), jnp.zeros((), BF16))
+
+
+def hot_columns(column, width):
+    rows = column.shape[0]
+    short = jnp.broadcast_to(column, (rows, LANES)).astype(I32).astype(jnp.int16)
+    at = lax.broadcasted_iota(jnp.int16, (rows, width), 1)
+    match = at == jnp.concatenate([short] * (width // LANES), axis=1)
+    return jnp.where(match, jnp.ones((), BF16), jnp.zeros((), BF16))
 
 
 def lanes_of(ref, first, count):
@@ -69,7 +84,7 @@
     count = ids.shape[1]
     lows, lines = table.shape
     line = ids >> 7
-    hot = ones_where(iota((lines, count), 0) == (line & (lines - 1)))
+    hot = hot_rows(lines, line & (lines - 1))
     low = (ids & 127) + jnp.where(line >= lines, LANES, 0)
     found = jnp.where(iota((lows, count), 0) == low, dot(table, hot), 0.0)
     return jnp.sum(found, axis=0, keepdims=True)
@@ -159,7 +174,7 @@
         mark[pl.ds(field * shards, shards), :] = base
         own, rank, base = rank_ids(owners[pl.ds(field, 1), :], base, shards, tri, ones)
         rank_scr[pl.ds(field, 1), :] = rank
-        at = ones_where(iota((width, count), 0, F32) == rank)
+        at = hot_rows(width, rank.astype(I32))
         return base, row + dot_nt((own * packed(ids, field)).astype(BF16), at)
 
     base, row = lax.fori_loop(
@@ -177,7 +192,7 @@
         base, row = carry
         ids = lanes_of(req_ref, c * batch, batch)
         own, rank, base = rank_ids(owners[pl.ds(fields + c, 1), :], base, shards, tri, ones)
-        at = ones_where(iota((LANES, count), 0, F32) == jnp.where(rank < REQ_SLOTS, rank, -1.0))
+        at = hot_rows(LANES, jnp.where(rank < REQ_SLOTS, rank, -1.0).astype(I32))
         field = c * (batch // per_field) + lane // (per_field * LANES)
         digits = [
             own * packed(ids, fields + c),
@@ -200,7 +215,7 @@
     ex[...] = jnp.zeros_like(ex)
     for kind, part in enumerate(parts):
         ex[pl.ds(kind, shards, stride=EXTRA), :] = part
-    extra_ref[...] = ex[...].astype(BF16)
+    extra_ref[...] = ex[: shards * EXTRA, :].astype(BF16)
     number = asked[2 * shards :]
     field = number.astype(I32) - 1
     mrow_ref[...] = jnp.where(
@@ -240,7 +255,7 @@
         source = jnp.concatenate(
             [jnp.where(block, sample, 0.0), jnp.where(block, field, 0.0)], axis=0
         ).astype(BF16)
-        col_ref[g] = dot_nt(ones_where(iota((LANES, total), 0) == (pos & 127)), source)
+        col_ref[g] = dot_nt(hot_rows(LANES, pos & 127), source)
         return unused
 
     lax.fori_loop(0, groups, group_step, 0, unroll=4)
@@ -251,7 +266,7 @@
     count = per_field * samples
     return [
         pltpu.VMEM((2 * LANES, lines // 2), BF16),
-        pltpu.VMEM((shards * EXTRA, LANES), F32),
+        pltpu.VMEM(((shards + 1) * EXTRA, LANES), F32),
         pltpu.VMEM((2 * fields, count), F32),
         pltpu.VMEM((2 * fields, count), F32),
         pltpu.VMEM((2 * fields, count), F32),
@@ -272,7 +287,7 @@
     def sort_group(g, unused):
         col = col_ref[g]
         hots = [
-            ones_where(iota((LANES, samples), 1, F32) == col[:, b : b + 1]) for b in range(blocks)
+            hot_columns(col[:, b : b + 1], samples) for b in range(blocks)
         ]
         part = grads_ref[:, pl.ds(pl.multiple_of(g * span, span), span)]
         rows = dot(jnp.concatenate(hots, axis=0), part)
@@ -320,7 +335,7 @@
 
     @pl.when(step == 0)
     def _():
-        scr[...] = extra_ref[...].astype(F32).reshape(scr.shape)
+        scr[: shards * EXTRA, :] = extra_ref[...].astype(F32).reshape(shards * EXTRA, LANES)
         kinds = [scr[pl.ds(kind, shards, stride=EXTRA), :] for kind in range(4)]
         first, last, unused = unpack(jnp.concatenate(kinds[:3], axis=0))
         first = jnp.maximum(first, 0.0).astype(I32)
@@ -341,13 +356,15 @@
     for k in range(group):
         for half in range(2):
             hi = hi_scr[half, pl.ds(step * group + k, 1), :]
-            highs.append(ones_where(iota((512, LANES), 0) == hi))
-            low = jnp.broadcast_to(
-                turned[:, half * shards + k : half * shards + k + 1], (LANES, LANES)
-            )
+            highs.append(hot_rows(512, hi))
+            low = turned[:, half * shards + k : half * shards + k + 1]
+            low = jnp.broadcast_to(low, (LANES, LANES)).astype(I32).astype(jnp.int16)
             rows = got_ref[k, half * LANES : (half + 1) * LANES, :]
+            zero = jnp.zeros((), BF16)
             values.append(
-                jnp.concatenate([rows * ones_where(low == float(q)) for q in range(4)], axis=1)
+                jnp.concatenate(
+                    [jnp.where(low == jnp.int16(q), rows, zero) for q in range(4)], axis=1
+                )
             )
     total[...] += dot(jnp.concatenate(highs, axis=1), jnp.concatenate(values, axis=0))
 
@@ -359,7 +376,7 @@
 
 def pick_rows(count, height, high, low, wide):
     hots = [
-        ones_where(iota((height, 512), 1, F32) == high[:height, b : b + 1]) for b in range(count)
+        hot_columns(high[:height, b : b + 1], 512) for b in range(count)
     ]
     rows = dot(jnp.concatenate(hots, axis=0), wide)
     lows = jnp.concatenate(
@@ -425,12 +442,13 @@
     hots, values = [], []
     for b in range(group):
         hots.append(
-            ones_where(iota((512, LANES), 0) == mrow_ref[pl.ds(step * group + b, 1), :])
+            hot_rows(512, mrow_ref[pl.ds(step * group + b, 1), :])
         )
-        low = jnp.broadcast_to(turned[:, b : b + 1], (LANES, LANES))
+        low = jnp.broadcast_to(turned[:, b : b + 1], (LANES, LANES)).astype(I32).astype(jnp.int16)
         rows = ret_ref[b, :LANES, :]
+        zero = jnp.zeros((), BF16)
         values.append(
-            jnp.concatenate([rows * (1.0 - low).astype(BF16), rows * low.astype(BF16)], axis=1)
+            jnp.concatenate([jnp.where(low == jnp.int16(q), rows, zero) for q in range(2)], axis=1)
         )
     total[...] += dot(jnp.concatenate(hots, axis=1), jnp.concatenate(values, axis=0))
     wide[step] = ret_ref[:, REQ_SLOTS:, :].reshape(wide.shape[1:])
@@ -452,7 +470,7 @@
         high = ((owner & 15) * 32 + last).astype(F32)
         zero = jnp.zeros((LANES // 2 - place.shape[0], LANES), F32)
         cols = jnp.concatenate([high, zero, (owner >> 4).astype(F32), zero], axis=0).T
-        moved = jnp.concatenate([wide[q] for q in range(4)], axis=1)
+        moved = jnp.concatenate([wide[q // 2, (q % 2) * 512 : (q % 2) * 512 + 512] for q in range(4)], axis=1)
         serving_ref[...] = pick_rows(
             place.shape[0], LANES, cols, cols[:, LANES // 2 :], moved
         )
@@ -529,7 +547,7 @@
     shape = jax.ShapeDtypeStruct
     extras = shape((shards * EXTRA, LANES), BF16)
     columns = shape((LANES, 2 * shards), F32)
-    ex = pltpu.VMEM(extras.shape, F32)
+    ex = pltpu.VMEM(((shards + 1) * EXTRA, LANES), F32)
 
     group = 16
     sent, mrow, mcol = call(
@@ -565,7 +583,7 @@
     )(*[in_hbm(array) for array in (sample_ids.T, places, req_ids.T, sample_grads)])
     got = exchange(sent)
 
-    group = 16
+    group = 32
     partial_sum, picks = call(
         functools.partial(sum_kernel, group),
         "gradient_sum",
@@ -587,7 +605,7 @@
     )(got, got)
     other = lax.ppermute(partial_sum, "rep", [(0, 1), (1, 0)])
 
-    group = 32
+    group = 64
     rows_type = shape((rows_dev, width), F32)
     any_space = pl.BlockSpec(memory_space=pl.ANY)
     new_rows, new_accum, sent, most = call(
@@ -629,7 +647,7 @@
     own_places = lax.dynamic_slice_in_dim(
         places, lax.axis_index("shard") * place_rows, place_rows, axis=0
     )
-    group = 16
+    group = 32
     scores, serving_rows = call(
         functools.partial(rank_kernel, group),
         "pool_rank",
@@ -649,7 +667,7 @@
         out_shape=(pltpu.HBM((1, requests), F32), shape((rows_dev, width), BF16)),
         scratch_shapes=[
             pltpu.VMEM((512, 256), F32),
-            pltpu.VMEM((4, 512, LANES), BF16),
+            pltpu.VMEM((2, 1024, LANES), BF16),
             pltpu.VMEM(w_hidden.shape, BF16),
             pltpu.SemaphoreType.DMA,
         ],

time: 151 us -> 146 us (0.967)
  Pallas kernels: 41.6 us -> 36.2 us
    pallas_call x1, Pallas kernels: 11.9 us -> 9.73 us  [on_device(): call(functools.partial(sum_kernel, group), 'gradient_sum', 2 ** 33, 2 **...]
    pallas_call x1, Pallas kernels: 17 us -> 15.3 us  [on_device(): call(functools.partial(send_kernel, shards, rows_dev, per_field, groups,...]
where the time goes in v4:
time: 146 us
  blocking collectives  66.8 us (46%)
  Pallas kernels  36.2 us (25%)
  waiting for transfers between devices  33.4 us (23%)
  starting transfers between devices  5.41 us (4%)
  local copies, waits for them, and re-layouts  2.4 us (2%)
    all_to_all x1, blocking collectives, exchange(): lax.all_to_all(rows, 'shard', split_axis=0, concat_axis=0, tiled=True)  66.8 us
    all_to_all x1, waiting for transfers between devices, exchange(): lax.all_to_all(rows, 'shard', split_axis=0, concat_axis=0, tiled=True)  30.7 us
    pallas_call x1, Pallas kernels, on_device(): call(functools.partial(send_kernel, shards, rows_dev, per_field, groups,...  15.3 us
    pallas_call x1, Pallas kernels, on_device(): call(functools.partial(sum_kernel, group), 'gradient_sum', 2 ** 33, 2 **...  9.73 us
    pallas_call x1, Pallas kernels, on_device(): call(functools.partial(update_kernel, group), 'update', 2 ** 32, 2 ** 23,...  5.69 us
    pallas_call x1, Pallas kernels, on_device(): call(functools.partial(rank_kernel, group), 'pool_rank', 2 ** 32, 2 ** 22...  5.53 us
    all_to_all x1, starting transfers between devices, exchange(): lax.all_to_all(rows, 'shard', split_axis=0, concat_axis=0, tiled=True)  5.15 us
  transfers between devices with their start and end apart: 2, of which 2 were waited for; matrix products, arithmetic and copies ran while one was open for 1% of the time, Pallas kernels for 0%

profile of v4, /device:TPU:0, one launch (start us, length us, event | category | flops | bytes accessed | tf_op | source)
XLA Modules:
  0.0 145.6 jit_solution(1036840365476942970)
XLA Ops:
  0.6 15.3 %send.1 = (bf16[64,272,128]{2,1,0:T(8,128)(2,1)S(1)}, s32[64,128]{1,0:T(8,128)S(1)}, f32[128,128]{1,0:T(8,128)S(1)}) custom-call(s32[32,256]{1,0:T(8,128)} %bitcast.49, s32[1024,128]{1,0:T(8,128)} %bitcast.47, s32[32,128]{1,0:T(8,128)} %bitcast.45, bf16[256,1024]{1,0:T(8,128)(2,1)} %grads_ref.1), custom_call_target="tpu_custom_call" | custom-call | flops 17179869184 | bytes 8388608 | tf_op jit(solution)/shard_map/send/pallas_call | solution.py:553
  15.9 66.8 %all_to_all.22.got_ref.extra_ref = bf16[64,272,128]{2,1,0:T(8,128)(2,1)S(1)} all-to-all(bf16[64,272,128]{2,1,0:T(8,128)(2,1)S(1)} %get-tuple-element.34), channel_id=1, replica_groups=mesh['rep'=2,'shard'=64] {'shard'}, dimensions={0} | all-to-all | bytes 8912896 | tf_op jit(solution)/shard_map/all_to_all | solution.py:521
  82.7 0.0 copy-start
  82.7 0.0 copy-start.1
  82.7 9.7 %gradient_sum.1 = (f32[2056,128]{1,0:T(8,128)S(1)}, f32[128,128]{1,0:T(8,128)S(1)}) custom-call(bf16[64,272,128]{2,1,0:T(8,128)(2,1)S(1)} %all_to_all.22.got_ref.extra_ref, bf16[64,272,128]{2,1,0:T(8,128)(2,1)S(1)} %all_to_all.22.got_ref.extra_ref), custom_call_target="tpu_custom_call" | custom-call | flops 8589934592 | bytes 4194304 | tf_op jit(solution)/shard_map/gradient_sum/pallas_call | solution.py:587
  92.5 0.3 collective-permute-start
  92.7 2.7 %collective-permute-done.two_ref = f32[2056,128]{1,0:T(8,128)S(1)} collective-permute-done((f32[2056,128]{1,0:T(8,128)S(1)}, f32[2056,128]{1,0:T(8,128)S(1)}, u32[]{:S(2)}, u32[]{:S(2)}) %collective-permute-start) | collective-permute-done | bytes 1052704 | tf_op jit(solution)/shard_map/ppermute | solution.py:606
  95.4 0.0 copy-done
  95.4 0.0 copy-done.1
  95.4 5.7 %update.1 = (f32[2048,128]{1,0:T(8,128)}, f32[2048,128]{1,0:T(8,128)}, bf16[64,144,128]{2,1,0:T(8,128)(2,1)}, f32[8,128]{1,0:T(8,128)S(1)}) custom-call(f32[2048,128]{1,0:T(8,128)S(1)} %copy-done, f32[2048,128]{1,0:T(8,128)S(1)} %copy-done.1, f32[2056,128]{1,0:T(8,128)S(1)} %get-tuple-element.35.one_ref, f32[2056,128]{1,0:T(8,128)S(1)} %collective-permute-done.two_ref, ...), custom_call_target="tpu_custom_call" | custom-call | flops 4294967296 | bytes 8388608 | tf_op jit(solution)/shard_map/update/pallas_call | solution.py:611
  101.1 0.0 copy-start.3
  101.1 0.0 copy-start.4
  101.1 5.1 %all-to-all-start.3 = ((bf16[64,144,128]{2,1,0:T(8,128)(2,1)}), bf16[64,144,128]{2,1,0:T(8,128)(2,1)S(1)}, u32[]{:S(2)}, u32[]{:S(2)}) async-start(bf16[64,144,128]{2,1,0:T(8,128)(2,1)} %get-tuple-element.39), calls=%async_computation.3 | async-start | bytes 4718592 | tf_op jit(solution)/shard_map/all_to_all | solution.py:521
  106.3 0.0 copy-done.3
  106.3 0.7 constant_dynamic-slice_fusion.place_ref
  107.0 0.5 slice.9
  108.2 30.7 %all-to-all-done.3.ret_ref = bf16[64,144,128]{2,1,0:T(8,128)(2,1)S(1)} async-done(((bf16[64,144,128]{2,1,0:T(8,128)(2,1)}), bf16[64,144,128]{2,1,0:T(8,128)(2,1)S(1)}, u32[]{:S(2)}, u32[]{:S(2)}) %all-to-all-start.3) | async-done | bytes 2359328 | tf_op jit(solution)/shard_map/all_to_all | solution.py:521
  138.9 0.0 copy-done.4
  138.9 0.0 copy-start.2
  138.9 5.5 %pool_rank.1 = (f32[1,128]{1,0:T(1,128)}, bf16[2048,128]{1,0:T(8,128)(2,1)}) custom-call(bf16[64,144,128]{2,1,0:T(8,128)(2,1)S(1)} %all-to-all-done.3.ret_ref, s32[64,128]{1,0:T(8,128)S(1)} %get-tuple-element.40.mrow_ref, f32[128,128]{1,0:T(8,128)S(1)} %get-tuple-element.41.mcol_ref, s32[16,128]{1,0:T(8,128)S(1)} %constant_dynamic-slice_fusion.place_ref, ...), custom_call_target="tpu_custom_call" | custom-call | flops 4294967296 | bytes 4194304 | tf_op jit(solution)/shard_map/pool_rank/pallas_call | solution.py:651
  144.4 0.0 copy-start.5
  144.5 0.0 copy-done.2
  144.5 0.6 copy-done.5
  145.1 0.0 copy-start.6
  145.1 0.5 copy-done.6
  (2 shorter events, 0.0 us)
Async XLA Ops:
  82.7 12.7 %copy-start = (f32[2048,128]{1,0:T(8,128)S(1)}, f32[2048,128]{1,0:T(8,128)}, u32[]{:S(2)}) copy-start(f32[2048,128]{1,0:T(8,128)} %table_ref.1) | copy-start | bytes 3145732
  82.7 12.7 %copy-start.1 = (f32[2048,128]{1,0:T(8,128)S(1)}, f32[2048,128]{1,0:T(8,128)}, u32[]{:S(2)}) copy-start(f32[2048,128]{1,0:T(8,128)} %accum_ref.1) | copy-start | bytes 3145732
  92.5 2.9 %collective-permute-start = (f32[2056,128]{1,0:T(8,128)S(1)}, f32[2056,128]{1,0:T(8,128)S(1)}, u32[]{:S(2)}, u32[]{:S(2)}) collective-permute-start(f32[2056,128]{1,0:T(8,128)S(1)} %get-tuple-element.35.one_ref), channel_id=1, source_target_pairs={{0,64},{64,0},{1,65},{65,1},{2,66},{66,2},{3,67},{67,3},{4,68},{68... | collective-permute-start | bytes 3158024 | tf_op jit(solution)/shard_map/ppermute | solution.py:606
  101.1 5.2 %copy-start.3 = (bf16[1024]{0:T(1024)(128)(2,1)S(1)}, bf16[1024]{0:T(1024)(128)(2,1)}, u32[]{:S(2)}) copy-start(bf16[1024]{0:T(1024)(128)(2,1)} %param.20) | copy-start | bytes 6148
  101.1 37.8 %copy-start.4 = (f32[1024]{0:T(1024)S(1)}, f32[1024]{0:T(1024)}, u32[]{:S(2)}) copy-start(f32[1024]{0:T(1024)} %param.19) | copy-start | bytes 12292
  101.1 37.8 %all-to-all-start.3 = ((bf16[64,144,128]{2,1,0:T(8,128)(2,1)}), bf16[64,144,128]{2,1,0:T(8,128)(2,1)S(1)}, u32[]{:S(2)}, u32[]{:S(2)}) async-start(bf16[64,144,128]{2,1,0:T(8,128)(2,1)} %get-tuple-element.39), calls=%async_computation.3 | async-start | bytes 4718592 | tf_op jit(solution)/shard_map/all_to_all | solution.py:521
  138.9 5.6 %copy-start.2 = (s32[128,32]{0,1:T(8,128)S(1)}, s32[128,32]{0,1:T(8,128)}, u32[]{:S(2)}) copy-start(s32[128,32]{0,1:T(8,128)} %param.17) | copy-start | bytes 49156
  144.4 0.7 copy-start.5
  145.1 0.5 copy-start.6

commit v5 on v4

--- a/solution.py
+++ b/solution.py
@@ -159,7 +159,7 @@
         return unused
 
     values[...] = jnp.zeros_like(values)
-    lax.fori_loop(0, fields, train_look_up, 0, unroll=4)
+    lax.fori_loop(0, fields, train_look_up, 0, unroll=8)
     lax.fori_loop(0, batches, request_look_up, 0, unroll=4)
     owner, unused, scale = unpack(values[...])
     owners[...] = owner
@@ -175,16 +175,18 @@
         own, rank, base = rank_ids(owners[pl.ds(field, 1), :], base, shards, tri, ones)
         rank_scr[pl.ds(field, 1), :] = rank
         at = hot_rows(width, rank.astype(I32))
-        return base, row + dot_nt((own * packed(ids, field)).astype(BF16), at)
+        digits = (own * packed(ids, field)).astype(BF16)
+        return base, row + dot_nt(at, jnp.concatenate([digits, digits], axis=0))
 
     base, row = lax.fori_loop(
         0,
         fields,
         field_step,
-        (jnp.zeros((shards, LANES), F32), jnp.zeros((shards, width), F32)),
-        unroll=4,
+        (jnp.zeros((shards, LANES), F32), jnp.zeros((width, 2 * shards), F32)),
+        unroll=8,
     )
     mark[fields * shards :, :] = base
+    row = row.T[:shards]
 
     lane = iota((1, count), 1)
 
@@ -304,7 +306,7 @@
         rows_scr[g, pad : pad + total, :] = picked
         return unused
 
-    lax.fori_loop(0, groups, sort_group, 0)
+    lax.fori_loop(0, groups, sort_group, 0, unroll=2)
 
 
 def fill_slots(step, group, groups, off_ref, extra_ref, rows_scr, out_ref):

time: 146 us -> 144 us (0.986)
  Pallas kernels: 36.2 us -> 33.9 us
    pallas_call x1, Pallas kernels: 15.3 us -> 13 us  [on_device(): call(functools.partial(send_kernel, shards, rows_dev, per_field, groups,...]
where the time goes in v5:
time: 144 us; the launch traced here: 143 us
  blocking collectives  66.8 us (46%)
  Pallas kernels  33.9 us (24%)
  waiting for transfers between devices  33.2 us (23%)
  starting transfers between devices  5.48 us (4%)
  local copies, waits for them, and re-layouts  2.4 us (2%)
    all_to_all x1, blocking collectives, exchange(): lax.all_to_all(rows, 'shard', split_axis=0, concat_axis=0, tiled=True)  66.8 us
    all_to_all x1, waiting for transfers between devices, exchange(): lax.all_to_all(rows, 'shard', split_axis=0, concat_axis=0, tiled=True)  30.5 us
    pallas_call x1, Pallas kernels, on_device(): call(functools.partial(send_kernel, shards, rows_dev, per_field, groups,...  13 us
    pallas_call x1, Pallas kernels, on_device(): call(functools.partial(sum_kernel, group), 'gradient_sum', 2 ** 33, 2 **...  9.73 us
    pallas_call x1, Pallas kernels, on_device(): call(functools.partial(update_kernel, group), 'update', 2 ** 32, 2 ** 23,...  5.69 us
    pallas_call x1, Pallas kernels, on_device(): call(functools.partial(rank_kernel, group), 'pool_rank', 2 ** 32, 2 ** 22...  5.54 us
    all_to_all x1, starting transfers between devices, exchange(): lax.all_to_all(rows, 'shard', split_axis=0, concat_axis=0, tiled=True)  5.4 us
  transfers between devices with their start and end apart: 2, of which 2 were waited for; matrix products, arithmetic and copies ran while one was open for 1% of the time, Pallas kernels for 0%

profile of v5, /device:TPU:0, one launch (start us, length us, event | category | flops | bytes accessed | tf_op | source)
XLA Modules:
  0.0 143.2 jit_solution(10885750146443286238)
XLA Ops:
  0.6 13.0 %send.1 = (bf16[64,272,128]{2,1,0:T(8,128)(2,1)S(1)}, s32[64,128]{1,0:T(8,128)S(1)}, f32[128,128]{1,0:T(8,128)S(1)}) custom-call(s32[32,256]{1,0:T(8,128)} %bitcast.49, s32[1024,128]{1,0:T(8,128)} %bitcast.47, s32[32,128]{1,0:T(8,128)} %bitcast.45, bf16[256,1024]{1,0:T(8,128)(2,1)} %grads_ref.1), custom_call_target="tpu_custom_call" | custom-call | flops 17179869184 | bytes 8388608 | tf_op jit(solution)/shard_map/send/pallas_call | solution.py:555
  13.6 66.8 %all_to_all.22.got_ref.extra_ref = bf16[64,272,128]{2,1,0:T(8,128)(2,1)S(1)} all-to-all(bf16[64,272,128]{2,1,0:T(8,128)(2,1)S(1)} %get-tuple-element.34), channel_id=1, replica_groups=mesh['rep'=2,'shard'=64] {'shard'}, dimensions={0} | all-to-all | bytes 8912896 | tf_op jit(solution)/shard_map/all_to_all | solution.py:523
  80.4 0.0 copy-start
  80.4 0.0 copy-start.1
  80.4 9.7 %gradient_sum.1 = (f32[2056,128]{1,0:T(8,128)S(1)}, f32[128,128]{1,0:T(8,128)S(1)}) custom-call(bf16[64,272,128]{2,1,0:T(8,128)(2,1)S(1)} %all_to_all.22.got_ref.extra_ref, bf16[64,272,128]{2,1,0:T(8,128)(2,1)S(1)} %all_to_all.22.got_ref.extra_ref), custom_call_target="tpu_custom_call" | custom-call | flops 8589934592 | bytes 4194304 | tf_op jit(solution)/shard_map/gradient_sum/pallas_call | solution.py:589
  90.2 0.1 collective-permute-start
  90.2 2.7 %collective-permute-done.two_ref = f32[2056,128]{1,0:T(8,128)S(1)} collective-permute-done((f32[2056,128]{1,0:T(8,128)S(1)}, f32[2056,128]{1,0:T(8,128)S(1)}, u32[]{:S(2)}, u32[]{:S(2)}) %collective-permute-start) | collective-permute-done | bytes 1052704 | tf_op jit(solution)/shard_map/ppermute | solution.py:608
  92.9 0.0 copy-done
  92.9 0.0 copy-done.1
  92.9 5.7 %update.1 = (f32[2048,128]{1,0:T(8,128)}, f32[2048,128]{1,0:T(8,128)}, bf16[64,144,128]{2,1,0:T(8,128)(2,1)}, f32[8,128]{1,0:T(8,128)S(1)}) custom-call(f32[2048,128]{1,0:T(8,128)S(1)} %copy-done, f32[2048,128]{1,0:T(8,128)S(1)} %copy-done.1, f32[2056,128]{1,0:T(8,128)S(1)} %get-tuple-element.35.one_ref, f32[2056,128]{1,0:T(8,128)S(1)} %collective-permute-done.two_ref, ...), custom_call_target="tpu_custom_call" | custom-call | flops 4294967296 | bytes 8388608 | tf_op jit(solution)/shard_map/update/pallas_call | solution.py:613
  98.6 0.0 copy-start.3
  98.6 0.0 copy-start.4
  98.6 5.4 %all-to-all-start.3 = ((bf16[64,144,128]{2,1,0:T(8,128)(2,1)}), bf16[64,144,128]{2,1,0:T(8,128)(2,1)S(1)}, u32[]{:S(2)}, u32[]{:S(2)}) async-start(bf16[64,144,128]{2,1,0:T(8,128)(2,1)} %get-tuple-element.39), calls=%async_computation.3 | async-start | bytes 4718592 | tf_op jit(solution)/shard_map/all_to_all | solution.py:523
  104.0 0.0 copy-done.3
  104.1 0.7 constant_dynamic-slice_fusion.place_ref
  104.8 0.5 slice.9
  105.9 30.5 %all-to-all-done.3.ret_ref = bf16[64,144,128]{2,1,0:T(8,128)(2,1)S(1)} async-done(((bf16[64,144,128]{2,1,0:T(8,128)(2,1)}), bf16[64,144,128]{2,1,0:T(8,128)(2,1)S(1)}, u32[]{:S(2)}, u32[]{:S(2)}) %all-to-all-start.3) | async-done | bytes 2359328 | tf_op jit(solution)/shard_map/all_to_all | solution.py:523
  136.4 0.0 copy-done.4
  136.4 0.0 copy-start.2
  136.4 5.5 %pool_rank.1 = (f32[1,128]{1,0:T(1,128)}, bf16[2048,128]{1,0:T(8,128)(2,1)}) custom-call(bf16[64,144,128]{2,1,0:T(8,128)(2,1)S(1)} %all-to-all-done.3.ret_ref, s32[64,128]{1,0:T(8,128)S(1)} %get-tuple-element.40.mrow_ref, f32[128,128]{1,0:T(8,128)S(1)} %get-tuple-element.41.mcol_ref, s32[16,128]{1,0:T(8,128)S(1)} %constant_dynamic-slice_fusion.place_ref, ...), custom_call_target="tpu_custom_call" | custom-call | flops 4294967296 | bytes 4194304 | tf_op jit(solution)/shard_map/pool_rank/pallas_call | solution.py:653
  142.0 0.0 copy-start.5
  142.0 0.0 copy-done.2
  142.0 0.6 copy-done.5
  142.6 0.0 copy-start.6
  142.7 0.5 copy-done.6
  (2 shorter events, 0.0 us)
Async XLA Ops:
  80.4 12.5 %copy-start = (f32[2048,128]{1,0:T(8,128)S(1)}, f32[2048,128]{1,0:T(8,128)}, u32[]{:S(2)}) copy-start(f32[2048,128]{1,0:T(8,128)} %table_ref.1) | copy-start | bytes 3145732
  80.4 12.5 %copy-start.1 = (f32[2048,128]{1,0:T(8,128)S(1)}, f32[2048,128]{1,0:T(8,128)}, u32[]{:S(2)}) copy-start(f32[2048,128]{1,0:T(8,128)} %accum_ref.1) | copy-start | bytes 3145732
  90.2 2.7 %collective-permute-start = (f32[2056,128]{1,0:T(8,128)S(1)}, f32[2056,128]{1,0:T(8,128)S(1)}, u32[]{:S(2)}, u32[]{:S(2)}) collective-permute-start(f32[2056,128]{1,0:T(8,128)S(1)} %get-tuple-element.35.one_ref), channel_id=1, source_target_pairs={{0,64},{64,0},{1,65},{65,1},{2,66},{66,2},{3,67},{67,3},{4,68},{68... | collective-permute-start | bytes 3158024 | tf_op jit(solution)/shard_map/ppermute | solution.py:608
  98.6 5.4 %copy-start.3 = (bf16[1024]{0:T(1024)(128)(2,1)S(1)}, bf16[1024]{0:T(1024)(128)(2,1)}, u32[]{:S(2)}) copy-start(bf16[1024]{0:T(1024)(128)(2,1)} %param.20) | copy-start | bytes 6148
  98.6 37.8 %copy-start.4 = (f32[1024]{0:T(1024)S(1)}, f32[1024]{0:T(1024)}, u32[]{:S(2)}) copy-start(f32[1024]{0:T(1024)} %param.19) | copy-start | bytes 12292
  98.6 37.8 %all-to-all-start.3 = ((bf16[64,144,128]{2,1,0:T(8,128)(2,1)}), bf16[64,144,128]{2,1,0:T(8,128)(2,1)S(1)}, u32[]{:S(2)}, u32[]{:S(2)}) async-start(bf16[64,144,128]{2,1,0:T(8,128)(2,1)} %get-tuple-element.39), calls=%async_computation.3 | async-start | bytes 4718592 | tf_op jit(solution)/shard_map/all_to_all | solution.py:523
  136.4 5.6 %copy-start.2 = (s32[128,32]{0,1:T(8,128)S(1)}, s32[128,32]{0,1:T(8,128)}, u32[]{:S(2)}) copy-start(s32[128,32]{0,1:T(8,128)} %param.17) | copy-start | bytes 49156
  142.0 0.7 copy-start.5
  142.6 0.5 copy-start.6

commit v6 on v5

--- a/solution.py
+++ b/solution.py
@@ -391,41 +391,39 @@
 
 
 def update_kernel(
-    group, table_ref, accum_ref, one_ref, two_ref, picks_ref, rows_ref, accum_out_ref, sent_ref,
-    most_ref, rows, updated, moved, wide, sems,
+    parts, table_ref, accum_ref, one_ref, two_ref, picks_ref, rows_ref, accum_out_ref, sent_ref,
+    most_ref, rows, updated, moved, sent, sems,
 ):
-    step = pl.program_id(0)
     count = rows.shape[0]
-    copies = (
+    most_ref[...] = jnp.maximum(one_ref[count:, :], two_ref[count:, :])
+    gradient = one_ref[:count, :] + two_ref[:count, :]
+    history = accum_ref[...] + gradient * gradient
+    updated[...] = history
+    rows[...] = table_ref[...] - 0.1 * gradient * lax.rsqrt(history)
+    copies = [
         pltpu.make_async_copy(rows, rows_ref, sems.at[0]),
         pltpu.make_async_copy(updated, accum_out_ref, sems.at[1]),
-    )
-
-    @pl.when(step == 0)
-    def _():
-        most_ref[...] = jnp.maximum(one_ref[count:, :], two_ref[count:, :])
-        gradient = one_ref[:count, :] + two_ref[:count, :]
-        history = accum_ref[...] + gradient * gradient
-        updated[...] = history
-        rows[...] = table_ref[...] - 0.1 * gradient * lax.rsqrt(history)
-        for copy in copies:
-            copy.start()
-        moved[...] = rows[...].astype(BF16)
-        wide[...] = jnp.concatenate(
-            [moved[q * 512 : (q + 1) * 512, :] for q in range(4)], axis=1
+    ]
+    for copy in copies:
+        copy.start()
+    moved[...] = rows[...].astype(BF16)
+    wide = jnp.concatenate([moved[q * 512 : (q + 1) * 512, :] for q in range(4)], axis=1)
+    shards = sent.shape[0]
+    block = count // shards
+    sent[:, REQ_SLOTS:, :] = moved[...].reshape(shards, block, LANES)
+    group = shards // parts
+    for part in range(parts):
+        first = part * group
+        picked = pick_rows(
+            group, REQ_SLOTS, picks_ref[:, first : first + group],
+            picks_ref[:, LANES // 2 + first : LANES // 2 + first + group], wide,
         )
-
-    turned = pltpu.roll(picks_ref[...], lax.rem(LANES - step * group, LANES), 1)
-    picked = pick_rows(group, REQ_SLOTS, turned, turned[:, LANES // 2 :], wide[...])
-    sent_ref[:, :REQ_SLOTS, :] = picked.reshape(group, REQ_SLOTS, LANES)
-    block = sent_ref.shape[1] - REQ_SLOTS
-    start = pl.multiple_of(step * (group * block), group * block)
-    sent_ref[:, REQ_SLOTS:, :] = moved[pl.ds(start, group * block), :].reshape(group, block, LANES)
-
-    @pl.when(step == pl.num_programs(0) - 1)
-    def _():
-        for copy in copies:
-            copy.wait()
+        at = slice(first, first + group)
+        sent[at, :REQ_SLOTS, :] = picked.reshape(group, REQ_SLOTS, LANES)
+        copies.append(pltpu.make_async_copy(sent.at[at], sent_ref.at[at], sems.at[2 + part]))
+        copies[-1].start()
+    for copy in copies:
+        copy.wait()
 
 
 def rank_kernel(
@@ -607,15 +605,15 @@
     )(got, got)
     other = lax.ppermute(partial_sum, "rep", [(0, 1), (1, 0)])
 
-    group = 64
+    parts = 4
+    any_space = pl.BlockSpec(memory_space=pl.ANY)
     rows_type = shape((rows_dev, width), F32)
-    any_space = pl.BlockSpec(memory_space=pl.ANY)
     new_rows, new_accum, sent, most = call(
-        functools.partial(update_kernel, group),
+        functools.partial(update_kernel, parts),
         "update",
         2**32,
         2**23,
-        grid=(shards // group,),
+        grid=(1,),
         in_specs=[
             whole(table_rows.shape),
             whole(accum.shape),
@@ -626,7 +624,7 @@
         out_specs=(
             any_space,
             any_space,
-            pl.BlockSpec((group, REQ_SLOTS + block, width), lambda g: (g, 0, 0)),
+            any_space,
             whole((8, LANES)),
         ),
         out_shape=(
@@ -639,8 +637,8 @@
             pltpu.VMEM(table_rows.shape, F32),
             pltpu.VMEM(table_rows.shape, F32),
             pltpu.VMEM(table_rows.shape, BF16),
-            pltpu.VMEM((512, 512), BF16),
-            pltpu.SemaphoreType.DMA((2,)),
+            pltpu.VMEM((shards, REQ_SLOTS + block, width), BF16),
+            pltpu.SemaphoreType.DMA((2 + parts,)),
         ],
     )(table_rows, accum, partial_sum, other, picks)
     returned = exchange(sent)

time: 144 us -> 143 us (level)
  no operation moved by 1% of the time
where the time goes in v6:
time: 143 us
  blocking collectives  66.8 us (47%)
  Pallas kernels  33.4 us (23%)
  waiting for transfers between devices  33.4 us (23%)
  starting transfers between devices  5.26 us (4%)
  local copies, waits for them, and re-layouts  2.4 us (2%)
    all_to_all x1, blocking collectives, exchange(): lax.all_to_all(rows, 'shard', split_axis=0, concat_axis=0, tiled=True)  66.8 us
    all_to_all x1, waiting for transfers between devices, exchange(): lax.all_to_all(rows, 'shard', split_axis=0, concat_axis=0, tiled=True)  30.7 us
    pallas_call x1, Pallas kernels, on_device(): call(functools.partial(send_kernel, shards, rows_dev, per_field, groups,...  13 us
    pallas_call x1, Pallas kernels, on_device(): call(functools.partial(sum_kernel, group), 'gradient_sum', 2 ** 33, 2 **...  9.73 us
    pallas_call x1, Pallas kernels, on_device(): call(functools.partial(rank_kernel, group), 'pool_rank', 2 ** 32, 2 ** 22...  5.53 us
    all_to_all x1, starting transfers between devices, exchange(): lax.all_to_all(rows, 'shard', split_axis=0, concat_axis=0, tiled=True)  5.18 us
    pallas_call x1, Pallas kernels, on_device(): call(functools.partial(update_kernel, parts), 'update', 2 ** 32, 2 ** 23,...  5.16 us
  transfers between devices with their start and end apart: 2, of which 2 were waited for; matrix products, arithmetic and copies ran while one was open for 1% of the time, Pallas kernels for 0%

profile of v6, /device:TPU:0, one launch (start us, length us, event | category | flops | bytes accessed | tf_op | source)
XLA Modules:
  0.0 142.6 jit_solution(6724870191805205126)
XLA Ops:
  0.6 13.0 %send.1 = (bf16[64,272,128]{2,1,0:T(8,128)(2,1)S(1)}, s32[64,128]{1,0:T(8,128)S(1)}, f32[128,128]{1,0:T(8,128)S(1)}) custom-call(s32[32,256]{1,0:T(8,128)} %bitcast.49, s32[1024,128]{1,0:T(8,128)} %bitcast.47, s32[32,128]{1,0:T(8,128)} %bitcast.45, bf16[256,1024]{1,0:T(8,128)(2,1)} %grads_ref.1), custom_call_target="tpu_custom_call" | custom-call | flops 17179869184 | bytes 8388608 | tf_op jit(solution)/shard_map/send/pallas_call | solution.py:553
  13.6 66.8 %all_to_all.22.got_ref.extra_ref = bf16[64,272,128]{2,1,0:T(8,128)(2,1)S(1)} all-to-all(bf16[64,272,128]{2,1,0:T(8,128)(2,1)S(1)} %get-tuple-element.34), channel_id=1, replica_groups=mesh['rep'=2,'shard'=64] {'shard'}, dimensions={0} | all-to-all | bytes 8912896 | tf_op jit(solution)/shard_map/all_to_all | solution.py:521
  80.4 0.0 copy-start
  80.4 0.0 copy-start.1
  80.4 9.7 %gradient_sum.1 = (f32[2056,128]{1,0:T(8,128)S(1)}, f32[128,128]{1,0:T(8,128)S(1)}) custom-call(bf16[64,272,128]{2,1,0:T(8,128)(2,1)S(1)} %all_to_all.22.got_ref.extra_ref, bf16[64,272,128]{2,1,0:T(8,128)(2,1)S(1)} %all_to_all.22.got_ref.extra_ref), custom_call_target="tpu_custom_call" | custom-call | flops 8589934592 | bytes 4194304 | tf_op jit(solution)/shard_map/gradient_sum/pallas_call | solution.py:587
  90.2 0.1 collective-permute-start
  90.2 2.7 %collective-permute-done.two_ref = f32[2056,128]{1,0:T(8,128)S(1)} collective-permute-done((f32[2056,128]{1,0:T(8,128)S(1)}, f32[2056,128]{1,0:T(8,128)S(1)}, u32[]{:S(2)}, u32[]{:S(2)}) %collective-permute-start) | collective-permute-done | bytes 1052704 | tf_op jit(solution)/shard_map/ppermute | solution.py:606
  92.9 0.0 copy-done
  92.9 0.0 copy-done.1
  92.9 5.2 %update.1 = (f32[2048,128]{1,0:T(8,128)}, f32[2048,128]{1,0:T(8,128)}, bf16[64,144,128]{2,1,0:T(8,128)(2,1)}, f32[8,128]{1,0:T(8,128)S(1)}) custom-call(f32[2048,128]{1,0:T(8,128)S(1)} %copy-done, f32[2048,128]{1,0:T(8,128)S(1)} %copy-done.1, f32[2056,128]{1,0:T(8,128)S(1)} %get-tuple-element.35.one_ref, f32[2056,128]{1,0:T(8,128)S(1)} %collective-permute-done.two_ref, ...), custom_call_target="tpu_custom_call" | custom-call | flops 4294967296 | bytes 8388608 | tf_op jit(solution)/shard_map/update/pallas_call | solution.py:611
  98.1 0.0 copy-start.3
  98.1 0.0 copy-start.4
  98.1 5.2 %all-to-all-start.3 = ((bf16[64,144,128]{2,1,0:T(8,128)(2,1)}), bf16[64,144,128]{2,1,0:T(8,128)(2,1)S(1)}, u32[]{:S(2)}, u32[]{:S(2)}) async-start(bf16[64,144,128]{2,1,0:T(8,128)(2,1)} %get-tuple-element.39), calls=%async_computation.3 | async-start | bytes 4718592 | tf_op jit(solution)/shard_map/all_to_all | solution.py:521
  103.3 0.0 copy-done.3
  103.3 0.7 constant_dynamic-slice_fusion.place_ref
  104.0 0.5 slice.9
  105.2 30.7 %all-to-all-done.3.ret_ref = bf16[64,144,128]{2,1,0:T(8,128)(2,1)S(1)} async-done(((bf16[64,144,128]{2,1,0:T(8,128)(2,1)}), bf16[64,144,128]{2,1,0:T(8,128)(2,1)S(1)}, u32[]{:S(2)}, u32[]{:S(2)}) %all-to-all-start.3) | async-done | bytes 2359328 | tf_op jit(solution)/shard_map/all_to_all | solution.py:521
  135.9 0.0 copy-done.4
  135.9 0.0 copy-start.2
  135.9 5.5 %pool_rank.1 = (f32[1,128]{1,0:T(1,128)}, bf16[2048,128]{1,0:T(8,128)(2,1)}) custom-call(bf16[64,144,128]{2,1,0:T(8,128)(2,1)S(1)} %all-to-all-done.3.ret_ref, s32[64,128]{1,0:T(8,128)S(1)} %get-tuple-element.40.mrow_ref, f32[128,128]{1,0:T(8,128)S(1)} %get-tuple-element.41.mcol_ref, s32[16,128]{1,0:T(8,128)S(1)} %constant_dynamic-slice_fusion.place_ref, ...), custom_call_target="tpu_custom_call" | custom-call | flops 4294967296 | bytes 4194304 | tf_op jit(solution)/shard_map/pool_rank/pallas_call | solution.py:651
  141.4 0.0 copy-start.5
  141.5 0.0 copy-done.2
  141.5 0.6 copy-done.5
  142.1 0.0 copy-start.6
  142.1 0.5 copy-done.6
  (2 shorter events, 0.0 us)
Async XLA Ops:
  80.4 12.5 %copy-start = (f32[2048,128]{1,0:T(8,128)S(1)}, f32[2048,128]{1,0:T(8,128)}, u32[]{:S(2)}) copy-start(f32[2048,128]{1,0:T(8,128)} %table_ref.1) | copy-start | bytes 3145732
  80.4 12.5 %copy-start.1 = (f32[2048,128]{1,0:T(8,128)S(1)}, f32[2048,128]{1,0:T(8,128)}, u32[]{:S(2)}) copy-start(f32[2048,128]{1,0:T(8,128)} %accum_ref.1) | copy-start | bytes 3145732
  90.2 2.7 %collective-permute-start = (f32[2056,128]{1,0:T(8,128)S(1)}, f32[2056,128]{1,0:T(8,128)S(1)}, u32[]{:S(2)}, u32[]{:S(2)}) collective-permute-start(f32[2056,128]{1,0:T(8,128)S(1)} %get-tuple-element.35.one_ref), channel_id=1, source_target_pairs={{0,64},{64,0},{1,65},{65,1},{2,66},{66,2},{3,67},{67,3},{4,68},{68... | collective-permute-start | bytes 3158024 | tf_op jit(solution)/shard_map/ppermute | solution.py:606
  98.1 5.2 %copy-start.3 = (bf16[1024]{0:T(1024)(128)(2,1)S(1)}, bf16[1024]{0:T(1024)(128)(2,1)}, u32[]{:S(2)}) copy-start(bf16[1024]{0:T(1024)(128)(2,1)} %param.20) | copy-start | bytes 6148
  98.1 37.8 %copy-start.4 = (f32[1024]{0:T(1024)S(1)}, f32[1024]{0:T(1024)}, u32[]{:S(2)}) copy-start(f32[1024]{0:T(1024)} %param.19) | copy-start | bytes 12292
  98.1 37.8 %all-to-all-start.3 = ((bf16[64,144,128]{2,1,0:T(8,128)(2,1)}), bf16[64,144,128]{2,1,0:T(8,128)(2,1)S(1)}, u32[]{:S(2)}, u32[]{:S(2)}) async-start(bf16[64,144,128]{2,1,0:T(8,128)(2,1)} %get-tuple-element.39), calls=%async_computation.3 | async-start | bytes 4718592 | tf_op jit(solution)/shard_map/all_to_all | solution.py:521
  135.9 5.6 %copy-start.2 = (s32[128,32]{0,1:T(8,128)S(1)}, s32[128,32]{0,1:T(8,128)}, u32[]{:S(2)}) copy-start(s32[128,32]{0,1:T(8,128)} %param.17) | copy-start | bytes 49156
  141.4 0.7 copy-start.5
  142.1 0.5 copy-start.6

commit v7 on v6

--- a/solution.py
+++ b/solution.py
@@ -351,7 +351,7 @@
             [high[2 * shards :].astype(F32), low[2 * shards :]], axis=0
         ).T
         most = jnp.max(kinds[3], axis=0, keepdims=True)
-        out_ref[4 * 512 :, :] = jnp.broadcast_to(most, (8, LANES))
+        out_ref[4 * 512 :, :] = jnp.broadcast_to(most, (16, LANES)).astype(BF16)
 
     turned = pltpu.roll(lo_scr[...], lax.rem(2 * shards - step * group, 2 * shards), 1)
     highs, values = [], []
@@ -373,7 +373,7 @@
     @pl.when(step == pl.num_programs(0) - 1)
     def _():
         for q in range(4):
-            out_ref[q * 512 : (q + 1) * 512, :] = total[:, q * LANES : (q + 1) * LANES]
+            out_ref[q * 512 : (q + 1) * 512, :] = total[:, q * LANES : (q + 1) * LANES].astype(BF16)
 
 
 def pick_rows(count, height, high, low, wide):
@@ -395,8 +395,9 @@
     most_ref, rows, updated, moved, sent, sems,
 ):
     count = rows.shape[0]
-    most_ref[...] = jnp.maximum(one_ref[count:, :], two_ref[count:, :])
-    gradient = one_ref[:count, :] + two_ref[:count, :]
+    most = jnp.maximum(one_ref[count:, :].astype(F32), two_ref[count:, :].astype(F32))
+    most_ref[...] = most[:8]
+    gradient = one_ref[:count, :].astype(F32) + two_ref[:count, :].astype(F32)
     history = accum_ref[...] + gradient * gradient
     updated[...] = history
     rows[...] = table_ref[...] - 0.1 * gradient * lax.rsqrt(history)
@@ -594,8 +595,8 @@
             pl.BlockSpec((group, slots + EXTRA, width), lambda g: (g, 0, 0)),
             pl.BlockSpec((shards, EXTRA, width), lambda g: (0, slots // EXTRA, 0)),
         ],
-        out_specs=(whole((rows_dev + 8, width)), whole(columns.shape)),
-        out_shape=(shape((rows_dev + 8, width), F32), columns),
+        out_specs=(whole((rows_dev + 16, width)), whole(columns.shape)),
+        out_shape=(shape((rows_dev + 16, width), BF16), columns),
         scratch_shapes=[
             ex,
             pltpu.VMEM((2, shards, LANES), I32),

time: 143 us -> 142 us (level)
  no operation moved by 1% of the time
where the time goes in v7:
time: 142 us
  blocking collectives  66.8 us (47%)
  Pallas kernels  33.4 us (24%)
  waiting for transfers between devices  32.6 us (23%)
  starting transfers between devices  5.33 us (4%)
  local copies, waits for them, and re-layouts  2.4 us (2%)
    all_to_all x1, blocking collectives, exchange(): lax.all_to_all(rows, 'shard', split_axis=0, concat_axis=0, tiled=True)  66.8 us
    all_to_all x1, waiting for transfers between devices, exchange(): lax.all_to_all(rows, 'shard', split_axis=0, concat_axis=0, tiled=True)  30.7 us
    pallas_call x1, Pallas kernels, on_device(): call(functools.partial(send_kernel, shards, rows_dev, per_field, groups,...  13 us
    pallas_call x1, Pallas kernels, on_device(): call(functools.partial(sum_kernel, group), 'gradient_sum', 2 ** 33, 2 **...  9.73 us
    pallas_call x1, Pallas kernels, on_device(): call(functools.partial(rank_kernel, group), 'pool_rank', 2 ** 32, 2 ** 22...  5.54 us
    all_to_all x1, starting transfers between devices, exchange(): lax.all_to_all(rows, 'shard', split_axis=0, concat_axis=0, tiled=True)  5.24 us
    pallas_call x1, Pallas kernels, on_device(): call(functools.partial(update_kernel, parts), 'update', 2 ** 32, 2 ** 23,...  5.17 us
  transfers between devices with their start and end apart: 2, of which 2 were waited for; matrix products, arithmetic and copies ran while one was open for 1% of the time, Pallas kernels for 0%

profile of v7, /device:TPU:0, one launch (start us, length us, event | category | flops | bytes accessed | tf_op | source)
XLA Modules:
  0.0 141.9 jit_solution(16806034824963648927)
XLA Ops:
  0.6 13.0 %send.1 = (bf16[64,272,128]{2,1,0:T(8,128)(2,1)S(1)}, s32[64,128]{1,0:T(8,128)S(1)}, f32[128,128]{1,0:T(8,128)S(1)}) custom-call(s32[32,256]{1,0:T(8,128)} %bitcast.49, s32[1024,128]{1,0:T(8,128)} %bitcast.47, s32[32,128]{1,0:T(8,128)} %bitcast.45, bf16[256,1024]{1,0:T(8,128)(2,1)} %grads_ref.1), custom_call_target="tpu_custom_call" | custom-call | flops 17179869184 | bytes 8388608 | tf_op jit(solution)/shard_map/send/pallas_call | solution.py:554
  13.6 66.8 %all_to_all.22.got_ref.extra_ref = bf16[64,272,128]{2,1,0:T(8,128)(2,1)S(1)} all-to-all(bf16[64,272,128]{2,1,0:T(8,128)(2,1)S(1)} %get-tuple-element.34), channel_id=1, replica_groups=mesh['rep'=2,'shard'=64] {'shard'}, dimensions={0} | all-to-all | bytes 8912896 | tf_op jit(solution)/shard_map/all_to_all | solution.py:522
  80.4 0.0 copy-start
  80.4 0.0 copy-start.1
  80.4 9.7 %gradient_sum.1 = (bf16[2064,128]{1,0:T(8,128)(2,1)S(1)}, f32[128,128]{1,0:T(8,128)S(1)}) custom-call(bf16[64,272,128]{2,1,0:T(8,128)(2,1)S(1)} %all_to_all.22.got_ref.extra_ref, bf16[64,272,128]{2,1,0:T(8,128)(2,1)S(1)} %all_to_all.22.got_ref.extra_ref), custom_call_target="tpu_custom_call" | custom-call | flops 8589934592 | bytes 4194304 | tf_op jit(solution)/shard_map/gradient_sum/pallas_call | solution.py:588
  90.2 0.1 collective-permute-start
  90.2 1.9 %collective-permute-done.two_ref = bf16[2064,128]{1,0:T(8,128)(2,1)S(1)} collective-permute-done((bf16[2064,128]{1,0:T(8,128)(2,1)S(1)}, bf16[2064,128]{1,0:T(8,128)(2,1)S(1)}, u32[]{:S(2)}, u32[]{:S(2)}) %collective-permute-start) | collective-permute-done | bytes 528416 | tf_op jit(solution)/shard_map/ppermute | solution.py:607
  92.1 0.0 copy-done
  92.2 0.0 copy-done.1
  92.2 5.2 %update.1 = (f32[2048,128]{1,0:T(8,128)}, f32[2048,128]{1,0:T(8,128)}, bf16[64,144,128]{2,1,0:T(8,128)(2,1)}, f32[8,128]{1,0:T(8,128)S(1)}) custom-call(f32[2048,128]{1,0:T(8,128)S(1)} %copy-done, f32[2048,128]{1,0:T(8,128)S(1)} %copy-done.1, bf16[2064,128]{1,0:T(8,128)(2,1)S(1)} %get-tuple-element.35.one_ref, ...), custom_call_target="tpu_custom_call" | custom-call | flops 4294967296 | bytes 8388608 | tf_op jit(solution)/shard_map/update/pallas_call | solution.py:612
  97.3 0.0 copy-start.3
  97.3 0.0 copy-start.4
  97.4 5.2 %all-to-all-start.3 = ((bf16[64,144,128]{2,1,0:T(8,128)(2,1)}), bf16[64,144,128]{2,1,0:T(8,128)(2,1)S(1)}, u32[]{:S(2)}, u32[]{:S(2)}) async-start(bf16[64,144,128]{2,1,0:T(8,128)(2,1)} %get-tuple-element.39), calls=%async_computation.3 | async-start | bytes 4718592 | tf_op jit(solution)/shard_map/all_to_all | solution.py:522
  102.6 0.0 copy-done.3
  102.6 0.7 constant_dynamic-slice_fusion.place_ref
  103.3 0.5 slice.9
  104.5 30.7 %all-to-all-done.3.ret_ref = bf16[64,144,128]{2,1,0:T(8,128)(2,1)S(1)} async-done(((bf16[64,144,128]{2,1,0:T(8,128)(2,1)}), bf16[64,144,128]{2,1,0:T(8,128)(2,1)S(1)}, u32[]{:S(2)}, u32[]{:S(2)}) %all-to-all-start.3) | async-done | bytes 2359328 | tf_op jit(solution)/shard_map/all_to_all | solution.py:522
  135.2 0.0 copy-done.4
  135.2 0.0 copy-start.2
  135.2 5.5 %pool_rank.1 = (f32[1,128]{1,0:T(1,128)}, bf16[2048,128]{1,0:T(8,128)(2,1)}) custom-call(bf16[64,144,128]{2,1,0:T(8,128)(2,1)S(1)} %all-to-all-done.3.ret_ref, s32[64,128]{1,0:T(8,128)S(1)} %get-tuple-element.40.mrow_ref, f32[128,128]{1,0:T(8,128)S(1)} %get-tuple-element.41.mcol_ref, s32[16,128]{1,0:T(8,128)S(1)} %constant_dynamic-slice_fusion.place_ref, ...), custom_call_target="tpu_custom_call" | custom-call | flops 4294967296 | bytes 4194304 | tf_op jit(solution)/shard_map/pool_rank/pallas_call | solution.py:652
  140.8 0.0 copy-start.5
  140.8 0.0 copy-done.2
  140.8 0.6 copy-done.5
  141.4 0.0 copy-start.6
  141.4 0.5 copy-done.6
  (2 shorter events, 0.0 us)
Async XLA Ops:
  80.4 11.7 %copy-start = (f32[2048,128]{1,0:T(8,128)S(1)}, f32[2048,128]{1,0:T(8,128)}, u32[]{:S(2)}) copy-start(f32[2048,128]{1,0:T(8,128)} %table_ref.1) | copy-start | bytes 3145732
  80.4 11.7 %copy-start.1 = (f32[2048,128]{1,0:T(8,128)S(1)}, f32[2048,128]{1,0:T(8,128)}, u32[]{:S(2)}) copy-start(f32[2048,128]{1,0:T(8,128)} %accum_ref.1) | copy-start | bytes 3145732
  90.2 2.0 %collective-permute-start = (bf16[2064,128]{1,0:T(8,128)(2,1)S(1)}, bf16[2064,128]{1,0:T(8,128)(2,1)S(1)}, u32[]{:S(2)}, u32[]{:S(2)}) collective-permute-start(bf16[2064,128]{1,0:T(8,128)(2,1)S(1)} %get-tuple-element.35.one_ref), channel_id=1, source_target_pairs={{0,64},{64,0},{1,65},{65,1},{2,66},{66,2},{3,67},{67,3},{4,68},{68... | collective-permute-start | bytes 1585160 | tf_op jit(solution)/shard_map/ppermute | solution.py:607
  97.3 5.3 %copy-start.3 = (bf16[1024]{0:T(1024)(128)(2,1)S(1)}, bf16[1024]{0:T(1024)(128)(2,1)}, u32[]{:S(2)}) copy-start(bf16[1024]{0:T(1024)(128)(2,1)} %param.20) | copy-start | bytes 6148
  97.3 37.9 %copy-start.4 = (f32[1024]{0:T(1024)S(1)}, f32[1024]{0:T(1024)}, u32[]{:S(2)}) copy-start(f32[1024]{0:T(1024)} %param.19) | copy-start | bytes 12292
  97.4 37.9 %all-to-all-start.3 = ((bf16[64,144,128]{2,1,0:T(8,128)(2,1)}), bf16[64,144,128]{2,1,0:T(8,128)(2,1)S(1)}, u32[]{:S(2)}, u32[]{:S(2)}) async-start(bf16[64,144,128]{2,1,0:T(8,128)(2,1)} %get-tuple-element.39), calls=%async_computation.3 | async-start | bytes 4718592 | tf_op jit(solution)/shard_map/all_to_all | solution.py:522
  135.2 5.6 %copy-start.2 = (s32[128,32]{0,1:T(8,128)S(1)}, s32[128,32]{0,1:T(8,128)}, u32[]{:S(2)}) copy-start(s32[128,32]{0,1:T(8,128)} %param.17) | copy-start | bytes 49156
  140.8 0.7 copy-start.5
  141.4 0.5 copy-start.6
